TPU v7x, 256 devices: a whole 4x4x8 slice. The times are simulated.
256 devices in a mesh: section: 8 (over z_lo, x), seq: 32 (over y, z_hi, core).
Axes of the slice: x: 4, y: 4, z: 8 (z_hi: 4, z_lo: 2; z = z_hi * 2 + z_lo), core: 2. Of those that a mesh axis runs over, the one named last changes fastest.
Arguments:
- latents: bfloat16 [4, 2048, 1024], P(None, 'seq'), may hold values from -6 to 6
- norm_gain: float32 [8, 1024], P('section'), may hold values from 0.1 to 1.9
- qkv_weight: bfloat16 [8, 1024, 3072], P('section', 'seq'), may hold values from -1 to 1
- proj_weight: bfloat16 [8, 1024, 1024], P('section', 'seq'), may hold values from -0.1875 to 0.1875
- merge_weight: bfloat16 [8, 1024, 1024], P('section', 'seq'), may hold values from -0.125 to 0.125
Outputs:
- denoised: bfloat16 [4, 2048, 1024], P(None, 'seq', 'section')
All inputs are finite; a program needn't handle non-finite values.
Results may differ from a plain program's by a relative error of at most 0.017.
Values may be sent and summed in bfloat16 or wider, within the bound.
A program may use at most 64 MiB of HBM per device.

v0:
```python
import jax
import jax.numpy as jnp
from jax import lax
from jax.sharding import PartitionSpec as P

HEADS = 16
HEAD_DIM = 64


EPSILON = 1e-05


def partner(value, axis, bit):
    mask = 2**bit
    pairs = [(source, source ^ mask) for source in range(lax.axis_size(axis))]
    return lax.ppermute(value, axis, pairs)


def shifted(value, axis, steps):
    count = lax.axis_size(axis)
    initial, last = (max(0, -steps), min(count, count - steps))
    return lax.ppermute(value, axis, [(source, source + steps) for source in range(initial, last)])


def layer_norm(hidden, gain_row):
    values = hidden.astype(jnp.float32)
    center = values - jnp.mean(values, axis=-1, keepdims=True)
    spread = jnp.mean(center * center, axis=-1, keepdims=True)
    return (center * lax.rsqrt(spread + EPSILON) * gain_row).astype(jnp.bfloat16)


def body(latents, norm_gain, qkv_weight, proj_weight, merge_weight):
    seq_count = lax.axis_size("seq")
    section_count = lax.axis_size("section")
    my_section = lax.axis_index("section")
    midpoint = section_count // 2
    windows = latents.shape[0]
    tok_rows = latents.shape[1]
    features = latents.shape[2]
    repeat = max(seq_count // HEADS, 1)
    groups = seq_count // repeat
    head_cols = features * repeat // seq_count
    per_device = head_cols // HEAD_DIM
    part_rows = tok_rows // repeat
    scale_factor = HEAD_DIM ** (-0.5)
    w_qkv, w_proj, w_merge = (
        lax.all_gather(qkv_weight, "seq", axis=1, tiled=True),
        lax.all_gather(proj_weight, "seq", axis=1, tiled=True),
        lax.all_gather(merge_weight, "seq", axis=1, tiled=True),
    )
    w_qkv = w_qkv[0]
    w_proj = w_proj[0]
    w_merge = w_merge[0]
    gain_row = norm_gain[0]
    decoder = my_section >= midpoint
    encoder = my_section < midpoint
    query_shape = (seq_count, part_rows * head_cols)
    key_shape = (seq_count, tok_rows * head_cols)

    def to_heads(array_in, spread_copies):
        if spread_copies:
            grouped = array_in.reshape(tok_rows, groups, head_cols).transpose(1, 0, 2)
            grouped = grouped.reshape(groups, 1, tok_rows * head_cols)
            grouped = jnp.broadcast_to(grouped, (groups, repeat, tok_rows * head_cols))
            return grouped.reshape(seq_count, tok_rows * head_cols)
        grouped = array_in.reshape(part_rows, repeat, groups, head_cols).transpose(2, 1, 0, 3)
        return grouped.reshape(seq_count, part_rows * head_cols)

    def from_heads(array_in):
        grouped = array_in.reshape(groups, repeat, part_rows, head_cols).transpose(2, 1, 0, 3)
        return grouped.reshape(tok_rows, features)

    def project(carried):
        normed = layer_norm(carried, gain_row)
        packed = jnp.dot(normed, w_qkv, preferred_element_type=jnp.float32).astype(jnp.bfloat16)
        return (
            to_heads(packed[:, :features], False),
            to_heads(packed[:, features : 2 * features], True),
            to_heads(packed[:, 2 * features :], True),
        )

    def spare_heads():
        return (
            jnp.zeros(query_shape, jnp.bfloat16),
            jnp.zeros(key_shape, jnp.bfloat16),
            jnp.zeros(key_shape, jnp.bfloat16),
        )

    def attend(queries, keys_in, values_in):
        query_rows = queries.reshape(-1, per_device, HEAD_DIM)
        key_rows = keys_in.reshape(-1, per_device, HEAD_DIM)
        value_rows = values_in.reshape(-1, per_device, HEAD_DIM)
        block_rows = min(512, query_rows.shape[0])
        blocked = query_rows.reshape(-1, block_rows, per_device, HEAD_DIM)

        def one_block(query_block):
            scores = (
                jnp.einsum(
                    "qhd,khd->hqk", query_block, key_rows, preferred_element_type=jnp.float32
                )
                * scale_factor
            )
            row_max = jnp.max(scores, axis=-1, keepdims=True)
            weights = jnp.exp(scores - row_max)
            totals = jnp.sum(weights, axis=-1)
            probs = weights.astype(jnp.bfloat16)
            mixed = jnp.einsum(
                "hqk,khd->qhd", probs, value_rows, preferred_element_type=jnp.float32
            )
            return (mixed / totals.T[:, :, None]).astype(jnp.bfloat16)

        return lax.map(one_block, blocked).reshape(query_shape)

    def mirror_each(skip_term):
        for bit_no in range(section_count.bit_length() - 1):
            skip_term = partner(skip_term, "section", bit_no)
        return skip_term

    def tick(tick_no, loop_state):
        incoming, skip_store, result = loop_state
        window_no = tick_no - my_section
        active = (window_no >= 0) & (window_no < windows)
        chosen = jnp.clip(window_no, 0, windows - 1)
        fresh = lax.dynamic_index_in_dim(latents, chosen, 0, keepdims=False)
        entering = jnp.where(my_section == 0, fresh, incoming)
        skip_slot = lax.dynamic_index_in_dim(skip_store, chosen, 0, keepdims=False)
        carried = lax.cond(
            active & decoder,
            lambda: (
                jnp.dot(entering, w_merge, preferred_element_type=jnp.float32)
                + skip_slot.astype(jnp.float32)
            ).astype(jnp.bfloat16),
            lambda: entering,
        )
        queries, keys_in, values_in = lax.cond(active, lambda: project(carried), spare_heads)
        queries, keys_in, values_in = (
            lax.all_to_all(queries, "seq", split_axis=0, concat_axis=0, tiled=True),
            lax.all_to_all(keys_in, "seq", split_axis=0, concat_axis=0, tiled=True),
            lax.all_to_all(values_in, "seq", split_axis=0, concat_axis=0, tiled=True),
        )
        attended = lax.cond(
            active,
            lambda: attend(queries, keys_in, values_in),
            lambda: jnp.zeros(query_shape, jnp.bfloat16),
        )
        attended = lax.all_to_all(attended, "seq", split_axis=0, concat_axis=0, tiled=True)
        leaving = lax.cond(
            active,
            lambda: (
                carried.astype(jnp.float32)
                + jnp.dot(from_heads(attended), w_proj, preferred_element_type=jnp.float32)
            ).astype(jnp.bfloat16),
            lambda: carried,
        )
        skip_term = lax.cond(
            active & encoder,
            lambda: jnp.dot(leaving, w_merge, preferred_element_type=jnp.float32).astype(
                jnp.bfloat16
            ),
            lambda: jnp.zeros_like(leaving),
        )
        arrived = mirror_each(skip_term)
        source_no = tick_no - (section_count - 1 - my_section)
        landing = decoder & (source_no >= 0) & (source_no < windows)
        target = jnp.clip(source_no, 0, windows - 1)
        updated = lax.dynamic_update_index_in_dim(skip_store, arrived, target, 0)
        skip_store = jnp.where(landing, updated, skip_store)
        incoming = shifted(leaving, "section", 1)
        finished = lax.dynamic_update_index_in_dim(result, leaving.astype(jnp.float32), chosen, 0)
        result = jnp.where(active & (my_section == section_count - 1), finished, result)
        return (incoming, skip_store, result)

    loop_state = (
        jnp.zeros(latents.shape[1:], jnp.bfloat16),
        jnp.zeros_like(latents),
        jnp.zeros(latents.shape, jnp.float32),
    )
    loop_state = lax.fori_loop(0, windows + section_count - 1, tick, loop_state)
    result = loop_state[2]
    return lax.psum_scatter(result.astype(jnp.bfloat16), "section", scatter_dimension=2, tiled=True)


def solution(mesh):
    placed = (
        P(None, "seq", None),
        P("section", None),
        P("section", "seq", None),
        P("section", "seq", None),
        P("section", "seq", None),
    )
    return jax.shard_map(
        body, mesh=mesh, in_specs=placed, out_specs=P(None, "seq", "section"), check_vma=False
    )
```

profile of v0, /device:TPU:8, one launch (start us, length us, event | category | flops | bytes accessed | tf_op | source)
XLA Modules:
  0.0 1418.4 jit_solution(8909768915828232268)
XLA Ops:
  8.8 57.5 %all-gather.4.cloned.1.call-done = bf16[1,1024,1024]{2,1,0:T(8,128)(2,1)} async-done(((bf16[1,32,1024]{2,1,0:T(8,128)(2,1)}), bf16[1,1024,1024]{2,1,0:T(8,128)(2,1)}) %all-gather.4.cloned.1.call-update) | async-done | bytes 2097168 | tf_op jit(solution)/shard_map/all_gather | solution.py:49
  66.3 54.3 %all-gather.8.cloned.1.call-done = bf16[1,1024,1024]{2,1,0:T(8,128)(2,1)} async-done(((bf16[1,32,1024]{2,1,0:T(8,128)(2,1)}), bf16[1,1024,1024]{2,1,0:T(8,128)(2,1)}) %all-gather.8.cloned.1.call-update) | async-done | bytes 2097168 | tf_op jit(solution)/shard_map/all_gather | solution.py:48
  120.7 69.7 %all-gather.6.cloned.1.call-done = bf16[1,1024,3072]{2,1,0:T(8,128)(2,1)} async-done(((bf16[1,32,3072]{2,1,0:T(8,128)(2,1)}), bf16[1,1024,3072]{2,1,0:T(8,128)(2,1)}) %all-gather.6.cloned.1.call-update) | async-done | bytes 6291472 | tf_op jit(solution)/shard_map/all_gather | solution.py:47
  191.3 1177.7 %while.28 = (s32[]{:T(128)}, bf16[64,1024]{1,0:T(8,128)(2,1)S(1)}, bf16[4,64,1024]{2,1,0:T(8,128)(2,1)S(1)}, bf16[4,64,1024]{2,1,0:T(8,128)(2,1)}, s32[]{:T(128)...) while((s32[]{:T(128)}, bf16[64,1024]{1,0:T(8,128)(2,1)S(1)}, ...), condition=%wide.region_17.18_spmd, body=%wide.region_0.17_spmd.sunk | while | flops 1083767808 | bytes 57427712 | solution.py:178
  224.3 8.1 all-to-all-done.1
  239.0 9.9 all-to-all-done.2
  249.1 11.3 conditional.13
  268.7 9.2 all-to-all-done.3
  330.2 8.1 all-to-all-done.1
  344.9 9.9 all-to-all-done.2
  355.1 11.3 conditional.13
  374.6 9.2 all-to-all-done.3
  436.6 8.1 all-to-all-done.1
  451.3 9.9 all-to-all-done.2
  461.5 11.3 conditional.13
  481.0 9.2 all-to-all-done.3
  542.5 8.1 all-to-all-done.1
  557.2 9.9 all-to-all-done.2
  567.4 11.3 conditional.13
  587.0 9.2 all-to-all-done.3
  641.9 8.1 all-to-all-done.1
  656.6 9.9 all-to-all-done.2
  675.0 9.2 all-to-all-done.3
  684.4 21.8 %collective-permute-start.1 = (bf16[64,1024]{1,0:T(8,128)(2,1)S(1)}, bf16[64,1024]{1,0:T(8,128)(2,1)S(1)}, u32[]{:S(2)}, u32[]{:S(2)}) collective-permute-start(bf16[64,1024]{1,0:T(8,128)(2,1)S(1)} %get-tuple-element.699), channel_id=1, source_target_pairs={{0,32},{32,0},{64,96},{96,64},{128,160},{160,128},{192,224},{224,1... | collective-permute-start | bytes 393224 | tf_op jit(solution)/shard_map/while/body/eval_jaxpr/ppermute | solution.py:16
  747.8 8.1 all-to-all-done.1
  762.5 9.9 all-to-all-done.2
  780.9 9.2 all-to-all-done.3
  796.4 25.3 %collective-permute-start.2 = (bf16[64,1024]{1,0:T(8,128)(2,1)S(1)}, bf16[64,1024]{1,0:T(8,128)(2,1)S(1)}, u32[]{:S(2)}, u32[]{:S(2)}) collective-permute-start(bf16[64,1024]{1,0:T(8,128)(2,1)S(1)} %collective-permute-done.1), channel_id=1, source_target_pairs={{0,64},{32,96},{64,0},{96,32},{128,192},{160,224},{192,128},{224,1... | collective-permute-start | bytes 393224 | tf_op jit(solution)/shard_map/while/body/eval_jaxpr/ppermute | solution.py:16
  855.3 8.1 all-to-all-done.1
  870.0 9.9 all-to-all-done.2
  888.4 9.2 all-to-all-done.3
  903.9 22.4 %collective-permute-start.2 = (bf16[64,1024]{1,0:T(8,128)(2,1)S(1)}, bf16[64,1024]{1,0:T(8,128)(2,1)S(1)}, u32[]{:S(2)}, u32[]{:S(2)}) collective-permute-start(bf16[64,1024]{1,0:T(8,128)(2,1)S(1)} %collective-permute-done.1), channel_id=1, source_target_pairs={{0,64},{32,96},{64,0},{96,32},{128,192},{160,224},{192,128},{224,1... | collective-permute-start | bytes 393224 | tf_op jit(solution)/shard_map/while/body/eval_jaxpr/ppermute | solution.py:16
  977.5 9.9 all-to-all-done.2
  995.9 9.2 all-to-all-done.3
  1018.3 24.6 %collective-permute-start.3 = (bf16[64,1024]{1,0:T(8,128)(2,1)S(1)}, bf16[64,1024]{1,0:T(8,128)(2,1)S(1)}, u32[]{:S(2)}, u32[]{:S(2)}) collective-permute-start(bf16[64,1024]{1,0:T(8,128)(2,1)S(1)} %collective-permute-done.2), channel_id=1, source_target_pairs={{0,128},{32,160},{64,192},{96,224},{128,0},{160,32},{192,64},{224,... | collective-permute-start | bytes 393224 | tf_op jit(solution)/shard_map/while/body/eval_jaxpr/ppermute | solution.py:16
  1071.2 9.4 all-to-all-done.1
  1086.9 10.7 all-to-all-done.2
  1106.4 9.4 all-to-all-done.3
  1129.6 20.4 %collective-permute-start.3 = (bf16[64,1024]{1,0:T(8,128)(2,1)S(1)}, bf16[64,1024]{1,0:T(8,128)(2,1)S(1)}, u32[]{:S(2)}, u32[]{:S(2)}) collective-permute-start(bf16[64,1024]{1,0:T(8,128)(2,1)S(1)} %collective-permute-done.2), channel_id=1, source_target_pairs={{0,128},{32,160},{64,192},{96,224},{128,0},{160,32},{192,64},{224,... | collective-permute-start | bytes 393224 | tf_op jit(solution)/shard_map/while/body/eval_jaxpr/ppermute | solution.py:16
  1177.6 9.4 all-to-all-done.1
  1193.3 11.1 all-to-all-done.2
  1212.8 9.2 all-to-all-done.3
  1235.4 22.4 %collective-permute-start.3 = (bf16[64,1024]{1,0:T(8,128)(2,1)S(1)}, bf16[64,1024]{1,0:T(8,128)(2,1)S(1)}, u32[]{:S(2)}, u32[]{:S(2)}) collective-permute-start(bf16[64,1024]{1,0:T(8,128)(2,1)S(1)} %collective-permute-done.2), channel_id=1, source_target_pairs={{0,128},{32,160},{64,192},{96,224},{128,0},{160,32},{192,64},{224,... | collective-permute-start | bytes 393224 | tf_op jit(solution)/shard_map/while/body/eval_jaxpr/ppermute | solution.py:16
  1285.4 9.4 all-to-all-done.1
  1301.2 11.1 all-to-all-done.2
  1320.7 9.2 all-to-all-done.3
  1344.5 21.5 %collective-permute-start.3 = (bf16[64,1024]{1,0:T(8,128)(2,1)S(1)}, bf16[64,1024]{1,0:T(8,128)(2,1)S(1)}, u32[]{:S(2)}, u32[]{:S(2)}) collective-permute-start(bf16[64,1024]{1,0:T(8,128)(2,1)S(1)} %collective-permute-done.2), channel_id=1, source_target_pairs={{0,128},{32,160},{64,192},{96,224},{128,0},{160,32},{192,64},{224,... | collective-permute-start | bytes 393224 | tf_op jit(solution)/shard_map/while/body/eval_jaxpr/ppermute | solution.py:16
  1372.1 38.0 %reduce-scatter.4.cloned.1.call-done = bf16[128,256]{1,0:T(8,128)(2,1)} async-done(((bf16[1024,256]{1,0:T(8,128)(2,1)}), bf16[128,256]{1,0:T(8,128)(2,1)}) %reduce-scatter.4.cloned.1.call-update) | async-done | bytes 65552
  (656 shorter events, 787.4 us)
Async XLA Ops:
  6.5 59.8 %all-gather.4.cloned.1.call-start = ((), (), s32[]{:S(2)}) async-start(), calls=%async_computation.5 | async-start | bytes 2162688 | tf_op jit(solution)/shard_map/all_gather | solution.py:49
  7.3 113.4 %all-gather.8.cloned.1.call-start = ((), (), s32[]{:S(2)}) async-start(), calls=%async_computation.7 | async-start | bytes 2162688 | tf_op jit(solution)/shard_map/all_gather | solution.py:48
  8.0 182.3 %all-gather.6.cloned.1.call-start = ((), (), s32[]{:S(2)}) async-start(), calls=%async_computation.6 | async-start | bytes 6488064 | tf_op jit(solution)/shard_map/all_gather | solution.py:47
  8.7 1401.4 %reduce-scatter.4.cloned.1.call-start = ((), (), s32[]{:S(2)}) async-start(), calls=%async_computation.8 | async-start | bytes 589824
  200.9 16.0 %all-to-all-start = ((bf16[32,2,1024]{2,1,0:T(2,128)(2,1)}), bf16[32,2,1024]{2,1,0:T(2,128)(2,1)S(1)}, u32[]{:S(2)}, u32[]{:S(2)}) async-start(bf16[32,2,1024]{2,1,0:T(2,128)(2,1)} %reshape.152), calls=%async_computation | async-start | bytes 262144 | tf_op jit(solution)/shard_map/while/body/eval_jaxpr/all_to_all | solution.py:137
  216.9 15.4 %all-to-all-start.1 = ((bf16[32,2,2048]{2,1,0:T(2,128)(2,1)}), bf16[32,2,2048]{2,1,0:T(2,128)(2,1)S(1)}, u32[]{:S(2)}, u32[]{:S(2)}) async-start(bf16[32,2,2048]{2,1,0:T(2,128)(2,1)} %reshape.154), calls=%async_computation.1 | async-start | bytes 524288 | tf_op jit(solution)/shard_map/while/body/eval_jaxpr/all_to_all | solution.py:138
  232.3 16.5 %all-to-all-start.2 = ((bf16[32,2,2048]{2,1,0:T(2,128)(2,1)}), bf16[32,2,2048]{2,1,0:T(2,128)(2,1)S(1)}, u32[]{:S(2)}, u32[]{:S(2)}) async-start(bf16[32,2,2048]{2,1,0:T(2,128)(2,1)} %reshape.156), calls=%async_computation.2 | async-start | bytes 524288 | tf_op jit(solution)/shard_map/while/body/eval_jaxpr/all_to_all | solution.py:139
  262.5 15.4 %all-to-all-start.3 = ((bf16[32,2,1024]{2,1,0:T(2,128)(2,1)}), bf16[32,2,1024]{2,1,0:T(2,128)(2,1)S(1)}, u32[]{:S(2)}, u32[]{:S(2)}) async-start(bf16[32,2,1024]{2,1,0:T(2,128)(2,1)} %reshape.158), calls=%async_computation.3 | async-start | bytes 262144 | tf_op jit(solution)/shard_map/while/body/eval_jaxpr/all_to_all | solution.py:146
  322.8 15.4 %all-to-all-start.1 = ((bf16[32,2,2048]{2,1,0:T(2,128)(2,1)}), bf16[32,2,2048]{2,1,0:T(2,128)(2,1)S(1)}, u32[]{:S(2)}, u32[]{:S(2)}) async-start(bf16[32,2,2048]{2,1,0:T(2,128)(2,1)} %reshape.154), calls=%async_computation.1 | async-start | bytes 524288 | tf_op jit(solution)/shard_map/while/body/eval_jaxpr/all_to_all | solution.py:138
  338.3 16.5 %all-to-all-start.2 = ((bf16[32,2,2048]{2,1,0:T(2,128)(2,1)}), bf16[32,2,2048]{2,1,0:T(2,128)(2,1)S(1)}, u32[]{:S(2)}, u32[]{:S(2)}) async-start(bf16[32,2,2048]{2,1,0:T(2,128)(2,1)} %reshape.156), calls=%async_computation.2 | async-start | bytes 524288 | tf_op jit(solution)/shard_map/while/body/eval_jaxpr/all_to_all | solution.py:139
  368.4 15.4 %all-to-all-start.3 = ((bf16[32,2,1024]{2,1,0:T(2,128)(2,1)}), bf16[32,2,1024]{2,1,0:T(2,128)(2,1)S(1)}, u32[]{:S(2)}, u32[]{:S(2)}) async-start(bf16[32,2,1024]{2,1,0:T(2,128)(2,1)} %reshape.158), calls=%async_computation.3 | async-start | bytes 262144 | tf_op jit(solution)/shard_map/while/body/eval_jaxpr/all_to_all | solution.py:146
  429.2 15.4 %all-to-all-start.1 = ((bf16[32,2,2048]{2,1,0:T(2,128)(2,1)}), bf16[32,2,2048]{2,1,0:T(2,128)(2,1)S(1)}, u32[]{:S(2)}, u32[]{:S(2)}) async-start(bf16[32,2,2048]{2,1,0:T(2,128)(2,1)} %reshape.154), calls=%async_computation.1 | async-start | bytes 524288 | tf_op jit(solution)/shard_map/while/body/eval_jaxpr/all_to_all | solution.py:138
  444.7 16.5 %all-to-all-start.2 = ((bf16[32,2,2048]{2,1,0:T(2,128)(2,1)}), bf16[32,2,2048]{2,1,0:T(2,128)(2,1)S(1)}, u32[]{:S(2)}, u32[]{:S(2)}) async-start(bf16[32,2,2048]{2,1,0:T(2,128)(2,1)} %reshape.156), calls=%async_computation.2 | async-start | bytes 524288 | tf_op jit(solution)/shard_map/while/body/eval_jaxpr/all_to_all | solution.py:139
  474.8 15.4 %all-to-all-start.3 = ((bf16[32,2,1024]{2,1,0:T(2,128)(2,1)}), bf16[32,2,1024]{2,1,0:T(2,128)(2,1)S(1)}, u32[]{:S(2)}, u32[]{:S(2)}) async-start(bf16[32,2,1024]{2,1,0:T(2,128)(2,1)} %reshape.158), calls=%async_computation.3 | async-start | bytes 262144 | tf_op jit(solution)/shard_map/while/body/eval_jaxpr/all_to_all | solution.py:146
  535.2 15.4 %all-to-all-start.1 = ((bf16[32,2,2048]{2,1,0:T(2,128)(2,1)}), bf16[32,2,2048]{2,1,0:T(2,128)(2,1)S(1)}, u32[]{:S(2)}, u32[]{:S(2)}) async-start(bf16[32,2,2048]{2,1,0:T(2,128)(2,1)} %reshape.154), calls=%async_computation.1 | async-start | bytes 524288 | tf_op jit(solution)/shard_map/while/body/eval_jaxpr/all_to_all | solution.py:138
  550.6 16.5 %all-to-all-start.2 = ((bf16[32,2,2048]{2,1,0:T(2,128)(2,1)}), bf16[32,2,2048]{2,1,0:T(2,128)(2,1)S(1)}, u32[]{:S(2)}, u32[]{:S(2)}) async-start(bf16[32,2,2048]{2,1,0:T(2,128)(2,1)} %reshape.156), calls=%async_computation.2 | async-start | bytes 524288 | tf_op jit(solution)/shard_map/while/body/eval_jaxpr/all_to_all | solution.py:139
  580.7 15.4 %all-to-all-start.3 = ((bf16[32,2,1024]{2,1,0:T(2,128)(2,1)}), bf16[32,2,1024]{2,1,0:T(2,128)(2,1)S(1)}, u32[]{:S(2)}, u32[]{:S(2)}) async-start(bf16[32,2,1024]{2,1,0:T(2,128)(2,1)} %reshape.158), calls=%async_computation.3 | async-start | bytes 262144 | tf_op jit(solution)/shard_map/while/body/eval_jaxpr/all_to_all | solution.py:146
  634.5 15.4 %all-to-all-start.1 = ((bf16[32,2,2048]{2,1,0:T(2,128)(2,1)}), bf16[32,2,2048]{2,1,0:T(2,128)(2,1)S(1)}, u32[]{:S(2)}, u32[]{:S(2)}) async-start(bf16[32,2,2048]{2,1,0:T(2,128)(2,1)} %reshape.154), calls=%async_computation.1 | async-start | bytes 524288 | tf_op jit(solution)/shard_map/while/body/eval_jaxpr/all_to_all | solution.py:138
  649.9 16.5 %all-to-all-start.2 = ((bf16[32,2,2048]{2,1,0:T(2,128)(2,1)}), bf16[32,2,2048]{2,1,0:T(2,128)(2,1)S(1)}, u32[]{:S(2)}, u32[]{:S(2)}) async-start(bf16[32,2,2048]{2,1,0:T(2,128)(2,1)} %reshape.156), calls=%async_computation.2 | async-start | bytes 524288 | tf_op jit(solution)/shard_map/while/body/eval_jaxpr/all_to_all | solution.py:139
  668.8 15.4 %all-to-all-start.3 = ((bf16[32,2,1024]{2,1,0:T(2,128)(2,1)}), bf16[32,2,1024]{2,1,0:T(2,128)(2,1)S(1)}, u32[]{:S(2)}, u32[]{:S(2)}) async-start(bf16[32,2,1024]{2,1,0:T(2,128)(2,1)} %reshape.158), calls=%async_computation.3 | async-start | bytes 262144 | tf_op jit(solution)/shard_map/while/body/eval_jaxpr/all_to_all | solution.py:146
  684.4 26.1 %collective-permute-start.1 = (bf16[64,1024]{1,0:T(8,128)(2,1)S(1)}, bf16[64,1024]{1,0:T(8,128)(2,1)S(1)}, u32[]{:S(2)}, u32[]{:S(2)}) collective-permute-start(bf16[64,1024]{1,0:T(8,128)(2,1)S(1)} %get-tuple-element.699), channel_id=1, source_target_pairs={{0,32},{32,0},{64,96},{96,64},{128,160},{160,128},{192,224},{224,1... | collective-permute-start | bytes 393224 | tf_op jit(solution)/shard_map/while/body/eval_jaxpr/ppermute | solution.py:16
  740.4 15.4 %all-to-all-start.1 = ((bf16[32,2,2048]{2,1,0:T(2,128)(2,1)}), bf16[32,2,2048]{2,1,0:T(2,128)(2,1)S(1)}, u32[]{:S(2)}, u32[]{:S(2)}) async-start(bf16[32,2,2048]{2,1,0:T(2,128)(2,1)} %reshape.154), calls=%async_computation.1 | async-start | bytes 524288 | tf_op jit(solution)/shard_map/while/body/eval_jaxpr/all_to_all | solution.py:138
  755.8 16.5 %all-to-all-start.2 = ((bf16[32,2,2048]{2,1,0:T(2,128)(2,1)}), bf16[32,2,2048]{2,1,0:T(2,128)(2,1)S(1)}, u32[]{:S(2)}, u32[]{:S(2)}) async-start(bf16[32,2,2048]{2,1,0:T(2,128)(2,1)} %reshape.156), calls=%async_computation.2 | async-start | bytes 524288 | tf_op jit(solution)/shard_map/while/body/eval_jaxpr/all_to_all | solution.py:139
  774.7 15.4 %all-to-all-start.3 = ((bf16[32,2,1024]{2,1,0:T(2,128)(2,1)}), bf16[32,2,1024]{2,1,0:T(2,128)(2,1)S(1)}, u32[]{:S(2)}, u32[]{:S(2)}) async-start(bf16[32,2,1024]{2,1,0:T(2,128)(2,1)} %reshape.158), calls=%async_computation.3 | async-start | bytes 262144 | tf_op jit(solution)/shard_map/while/body/eval_jaxpr/all_to_all | solution.py:146
  796.4 29.4 %collective-permute-start.2 = (bf16[64,1024]{1,0:T(8,128)(2,1)S(1)}, bf16[64,1024]{1,0:T(8,128)(2,1)S(1)}, u32[]{:S(2)}, u32[]{:S(2)}) collective-permute-start(bf16[64,1024]{1,0:T(8,128)(2,1)S(1)} %collective-permute-done.1), channel_id=1, source_target_pairs={{0,64},{32,96},{64,0},{96,32},{128,192},{160,224},{192,128},{224,1... | collective-permute-start | bytes 393224 | tf_op jit(solution)/shard_map/while/body/eval_jaxpr/ppermute | solution.py:16
  847.9 15.4 %all-to-all-start.1 = ((bf16[32,2,2048]{2,1,0:T(2,128)(2,1)}), bf16[32,2,2048]{2,1,0:T(2,128)(2,1)S(1)}, u32[]{:S(2)}, u32[]{:S(2)}) async-start(bf16[32,2,2048]{2,1,0:T(2,128)(2,1)} %reshape.154), calls=%async_computation.1 | async-start | bytes 524288 | tf_op jit(solution)/shard_map/while/body/eval_jaxpr/all_to_all | solution.py:138
  863.4 16.5 %all-to-all-start.2 = ((bf16[32,2,2048]{2,1,0:T(2,128)(2,1)}), bf16[32,2,2048]{2,1,0:T(2,128)(2,1)S(1)}, u32[]{:S(2)}, u32[]{:S(2)}) async-start(bf16[32,2,2048]{2,1,0:T(2,128)(2,1)} %reshape.156), calls=%async_computation.2 | async-start | bytes 524288 | tf_op jit(solution)/shard_map/while/body/eval_jaxpr/all_to_all | solution.py:139
  882.2 15.4 %all-to-all-start.3 = ((bf16[32,2,1024]{2,1,0:T(2,128)(2,1)}), bf16[32,2,1024]{2,1,0:T(2,128)(2,1)S(1)}, u32[]{:S(2)}, u32[]{:S(2)}) async-start(bf16[32,2,1024]{2,1,0:T(2,128)(2,1)} %reshape.158), calls=%async_computation.3 | async-start | bytes 262144 | tf_op jit(solution)/shard_map/while/body/eval_jaxpr/all_to_all | solution.py:146
  903.9 26.1 %collective-permute-start.2 = (bf16[64,1024]{1,0:T(8,128)(2,1)S(1)}, bf16[64,1024]{1,0:T(8,128)(2,1)S(1)}, u32[]{:S(2)}, u32[]{:S(2)}) collective-permute-start(bf16[64,1024]{1,0:T(8,128)(2,1)S(1)} %collective-permute-done.1), channel_id=1, source_target_pairs={{0,64},{32,96},{64,0},{96,32},{128,192},{160,224},{192,128},{224,1... | collective-permute-start | bytes 393224 | tf_op jit(solution)/shard_map/while/body/eval_jaxpr/ppermute | solution.py:16
  955.4 15.4 %all-to-all-start.1 = ((bf16[32,2,2048]{2,1,0:T(2,128)(2,1)}), bf16[32,2,2048]{2,1,0:T(2,128)(2,1)S(1)}, u32[]{:S(2)}, u32[]{:S(2)}) async-start(bf16[32,2,2048]{2,1,0:T(2,128)(2,1)} %reshape.154), calls=%async_computation.1 | async-start | bytes 524288 | tf_op jit(solution)/shard_map/while/body/eval_jaxpr/all_to_all | solution.py:138
  970.9 16.5 %all-to-all-start.2 = ((bf16[32,2,2048]{2,1,0:T(2,128)(2,1)}), bf16[32,2,2048]{2,1,0:T(2,128)(2,1)S(1)}, u32[]{:S(2)}, u32[]{:S(2)}) async-start(bf16[32,2,2048]{2,1,0:T(2,128)(2,1)} %reshape.156), calls=%async_computation.2 | async-start | bytes 524288 | tf_op jit(solution)/shard_map/while/body/eval_jaxpr/all_to_all | solution.py:139
  989.7 15.4 %all-to-all-start.3 = ((bf16[32,2,1024]{2,1,0:T(2,128)(2,1)}), bf16[32,2,1024]{2,1,0:T(2,128)(2,1)S(1)}, u32[]{:S(2)}, u32[]{:S(2)}) async-start(bf16[32,2,1024]{2,1,0:T(2,128)(2,1)} %reshape.158), calls=%async_computation.3 | async-start | bytes 262144 | tf_op jit(solution)/shard_map/while/body/eval_jaxpr/all_to_all | solution.py:146
  1013.8 32.1 %collective-permute-start = (bf16[64,1024]{1,0:T(8,128)(2,1)S(1)}, bf16[64,1024]{1,0:T(8,128)(2,1)S(1)}, u32[]{:S(2)}, u32[]{:S(2)}) collective-permute-start(bf16[64,1024]{1,0:T(8,128)(2,1)S(1)} %get-tuple-element.591), channel_id=1, source_target_pairs={{0,32},{32,64},{64,96},{96,128},{128,160},{160,192},{192,224},{1,3... | collective-permute-start | bytes 393224 | tf_op jit(solution)/shard_map/while/body/eval_jaxpr/ppermute | solution.py:22
  1018.3 27.5 %collective-permute-start.3 = (bf16[64,1024]{1,0:T(8,128)(2,1)S(1)}, bf16[64,1024]{1,0:T(8,128)(2,1)S(1)}, u32[]{:S(2)}, u32[]{:S(2)}) collective-permute-start(bf16[64,1024]{1,0:T(8,128)(2,1)S(1)} %collective-permute-done.2), channel_id=1, source_target_pairs={{0,128},{32,160},{64,192},{96,224},{128,0},{160,32},{192,64},{224,... | collective-permute-start | bytes 393224 | tf_op jit(solution)/shard_map/while/body/eval_jaxpr/ppermute | solution.py:16
  1063.1 17.5 %all-to-all-start.1 = ((bf16[32,2,2048]{2,1,0:T(2,128)(2,1)}), bf16[32,2,2048]{2,1,0:T(2,128)(2,1)S(1)}, u32[]{:S(2)}, u32[]{:S(2)}) async-start(bf16[32,2,2048]{2,1,0:T(2,128)(2,1)} %reshape.154), calls=%async_computation.1 | async-start | bytes 524288 | tf_op jit(solution)/shard_map/while/body/eval_jaxpr/all_to_all | solution.py:138
  1080.6 17.1 %all-to-all-start.2 = ((bf16[32,2,2048]{2,1,0:T(2,128)(2,1)}), bf16[32,2,2048]{2,1,0:T(2,128)(2,1)S(1)}, u32[]{:S(2)}, u32[]{:S(2)}) async-start(bf16[32,2,2048]{2,1,0:T(2,128)(2,1)} %reshape.156), calls=%async_computation.2 | async-start | bytes 524288 | tf_op jit(solution)/shard_map/while/body/eval_jaxpr/all_to_all | solution.py:139
  1100.0 15.7 %all-to-all-start.3 = ((bf16[32,2,1024]{2,1,0:T(2,128)(2,1)}), bf16[32,2,1024]{2,1,0:T(2,128)(2,1)S(1)}, u32[]{:S(2)}, u32[]{:S(2)}) async-start(bf16[32,2,1024]{2,1,0:T(2,128)(2,1)} %reshape.158), calls=%async_computation.3 | async-start | bytes 262144 | tf_op jit(solution)/shard_map/while/body/eval_jaxpr/all_to_all | solution.py:146
  1122.3 30.7 %collective-permute-start = (bf16[64,1024]{1,0:T(8,128)(2,1)S(1)}, bf16[64,1024]{1,0:T(8,128)(2,1)S(1)}, u32[]{:S(2)}, u32[]{:S(2)}) collective-permute-start(bf16[64,1024]{1,0:T(8,128)(2,1)S(1)} %get-tuple-element.591), channel_id=1, source_target_pairs={{0,32},{32,64},{64,96},{96,128},{128,160},{160,192},{192,224},{1,3... | collective-permute-start | bytes 393224 | tf_op jit(solution)/shard_map/while/body/eval_jaxpr/ppermute | solution.py:22
  1129.6 23.3 %collective-permute-start.3 = (bf16[64,1024]{1,0:T(8,128)(2,1)S(1)}, bf16[64,1024]{1,0:T(8,128)(2,1)S(1)}, u32[]{:S(2)}, u32[]{:S(2)}) collective-permute-start(bf16[64,1024]{1,0:T(8,128)(2,1)S(1)} %collective-permute-done.2), channel_id=1, source_target_pairs={{0,128},{32,160},{64,192},{96,224},{128,0},{160,32},{192,64},{224,... | collective-permute-start | bytes 393224 | tf_op jit(solution)/shard_map/while/body/eval_jaxpr/ppermute | solution.py:16
  1170.2 16.8 %all-to-all-start.1 = ((bf16[32,2,2048]{2,1,0:T(2,128)(2,1)}), bf16[32,2,2048]{2,1,0:T(2,128)(2,1)S(1)}, u32[]{:S(2)}, u32[]{:S(2)}) async-start(bf16[32,2,2048]{2,1,0:T(2,128)(2,1)} %reshape.154), calls=%async_computation.1 | async-start | bytes 524288 | tf_op jit(solution)/shard_map/while/body/eval_jaxpr/all_to_all | solution.py:138
  1187.0 17.4 %all-to-all-start.2 = ((bf16[32,2,2048]{2,1,0:T(2,128)(2,1)}), bf16[32,2,2048]{2,1,0:T(2,128)(2,1)S(1)}, u32[]{:S(2)}, u32[]{:S(2)}) async-start(bf16[32,2,2048]{2,1,0:T(2,128)(2,1)} %reshape.156), calls=%async_computation.2 | async-start | bytes 524288 | tf_op jit(solution)/shard_map/while/body/eval_jaxpr/all_to_all | solution.py:139
  1206.8 15.3 %all-to-all-start.3 = ((bf16[32,2,1024]{2,1,0:T(2,128)(2,1)}), bf16[32,2,1024]{2,1,0:T(2,128)(2,1)S(1)}, u32[]{:S(2)}, u32[]{:S(2)}) async-start(bf16[32,2,1024]{2,1,0:T(2,128)(2,1)} %reshape.158), calls=%async_computation.3 | async-start | bytes 262144 | tf_op jit(solution)/shard_map/while/body/eval_jaxpr/all_to_all | solution.py:146
  1229.9 31.0 %collective-permute-start = (bf16[64,1024]{1,0:T(8,128)(2,1)S(1)}, bf16[64,1024]{1,0:T(8,128)(2,1)S(1)}, u32[]{:S(2)}, u32[]{:S(2)}) collective-permute-start(bf16[64,1024]{1,0:T(8,128)(2,1)S(1)} %get-tuple-element.591), channel_id=1, source_target_pairs={{0,32},{32,64},{64,96},{96,128},{128,160},{160,192},{192,224},{1,3... | collective-permute-start | bytes 393224 | tf_op jit(solution)/shard_map/while/body/eval_jaxpr/ppermute | solution.py:22
  1235.4 25.4 %collective-permute-start.3 = (bf16[64,1024]{1,0:T(8,128)(2,1)S(1)}, bf16[64,1024]{1,0:T(8,128)(2,1)S(1)}, u32[]{:S(2)}, u32[]{:S(2)}) collective-permute-start(bf16[64,1024]{1,0:T(8,128)(2,1)S(1)} %collective-permute-done.2), channel_id=1, source_target_pairs={{0,128},{32,160},{64,192},{96,224},{128,0},{160,32},{192,64},{224,... | collective-permute-start | bytes 393224 | tf_op jit(solution)/shard_map/while/body/eval_jaxpr/ppermute | solution.py:16
  1278.1 16.8 %all-to-all-start.1 = ((bf16[32,2,2048]{2,1,0:T(2,128)(2,1)}), bf16[32,2,2048]{2,1,0:T(2,128)(2,1)S(1)}, u32[]{:S(2)}, u32[]{:S(2)}) async-start(bf16[32,2,2048]{2,1,0:T(2,128)(2,1)} %reshape.154), calls=%async_computation.1 | async-start | bytes 524288 | tf_op jit(solution)/shard_map/while/body/eval_jaxpr/all_to_all | solution.py:138
  1294.9 17.4 %all-to-all-start.2 = ((bf16[32,2,2048]{2,1,0:T(2,128)(2,1)}), bf16[32,2,2048]{2,1,0:T(2,128)(2,1)S(1)}, u32[]{:S(2)}, u32[]{:S(2)}) async-start(bf16[32,2,2048]{2,1,0:T(2,128)(2,1)} %reshape.156), calls=%async_computation.2 | async-start | bytes 524288 | tf_op jit(solution)/shard_map/while/body/eval_jaxpr/all_to_all | solution.py:139
  1340.6 28.4 %collective-permute-start = (bf16[64,1024]{1,0:T(8,128)(2,1)S(1)}, bf16[64,1024]{1,0:T(8,128)(2,1)S(1)}, u32[]{:S(2)}, u32[]{:S(2)}) collective-permute-start(bf16[64,1024]{1,0:T(8,128)(2,1)S(1)} %get-tuple-element.591), channel_id=1, source_target_pairs={{0,32},{32,64},{64,96},{96,128},{128,160},{160,192},{192,224},{1,3... | collective-permute-start | bytes 393224 | tf_op jit(solution)/shard_map/while/body/eval_jaxpr/ppermute | solution.py:22
  1344.5 24.5 %collective-permute-start.3 = (bf16[64,1024]{1,0:T(8,128)(2,1)S(1)}, bf16[64,1024]{1,0:T(8,128)(2,1)S(1)}, u32[]{:S(2)}, u32[]{:S(2)}) collective-permute-start(bf16[64,1024]{1,0:T(8,128)(2,1)S(1)} %collective-permute-done.2), channel_id=1, source_target_pairs={{0,128},{32,160},{64,192},{96,224},{128,0},{160,32},{192,64},{224,... | collective-permute-start | bytes 393224 | tf_op jit(solution)/shard_map/while/body/eval_jaxpr/ppermute | solution.py:16
  (55 other events, 600.0 us)
Sparse Core Ops, SparseCore 0:
  9.9 56.3 all-gather.3
  68.9 51.7 all-gather.7
  123.2 67.0 all-gather.5
  1372.2 37.8 reduce-scatter.3
where the time goes:
time: 1420 us
  waiting for transfers between devices  724 us (51%)
  starting transfers between devices  458 us (32%)
  local copies, waits for them, and re-layouts  95.2 us (7%)
  other arithmetic  83.3 us (6%)
  matrix products  40.5 us (3%)
    ppermute x33, starting transfers between devices, partner(): return lax.ppermute(value, axis, pairs)  187 us
    ppermute x33, waiting for transfers between devices, partner(): return lax.ppermute(value, axis, pairs)  119 us
    all_to_all x11, waiting for transfers between devices, tick(): lax.all_to_all(values_in, 'seq', split_axis=0, concat_axis=0, tiled=True)  112 us
    all_to_all x11, waiting for transfers between devices, tick(): lax.all_to_all(attended, 'seq', split_axis=0, concat_axis=0, tiled=True)  102 us
    all_to_all x11, waiting for transfers between devices, tick(): lax.all_to_all(keys_in, 'seq', split_axis=0, concat_axis=0, tiled=True)  92.7 us
    all_to_all x11, waiting for transfers between devices, tick(): lax.all_to_all(queries, 'seq', split_axis=0, concat_axis=0, tiled=True)  76.6 us
    all_gather x1, waiting for transfers between devices, body(): lax.all_gather(qkv_weight, 'seq', axis=1, tiled=True)  69.7 us
    all_to_all x11, starting transfers between devices, tick(): lax.all_to_all(attended, 'seq', split_axis=0, concat_axis=0, tiled=True)  68 us
  transfers between devices with their start and end apart: 92, of which 81 were waited for; matrix products, arithmetic and copies ran while one was open for 5% of the time, Pallas kernels for 0%

commit v1 on v0

v1 whole, which is shorter than its diff:
```python
import functools
import math

import jax
import jax.numpy as jnp
from jax import lax
from jax.experimental import pallas as pl
from jax.experimental.pallas import tpu as pltpu
from jax.sharding import PartitionSpec as P

HEAD_DIM = 64
SLICE = 128
CORES = 2
EPSILON = 1e-05
F32 = jnp.float32
BF16 = jnp.bfloat16


def rcopy(src, dst, send, recv, section, seq):
    return pltpu.make_async_remote_copy(
        src_ref=src,
        dst_ref=dst,
        send_sem=send,
        recv_sem=recv,
        device_id={"section": section, "seq": seq},
        device_id_type=pl.DeviceIdType.MESH,
    )


def kernel(ns, ny, nz, tok, lat_ref, w_ref, out_ref, H, U, A, KV, S, W, skips, O,
           p1s, p1r, zs, zr, ys, yr, cs, cr, hs, hr, us, ur, as_, ar, kvs, kvr, os_, or_):
    nc = CORES
    rows = nz * tok
    nt = ny * nc
    dim = ns * SLICE
    sec = lax.axis_index("section")
    seq = lax.axis_index("seq")
    y = seq // (nz * nc)
    z = (seq // nc) % nz
    c = seq % nc
    t = y * nc + c

    def seq_of(y_, z_, c_):
        return y_ * (nz * nc) + z_ * nc + c_

    def sec_peer(d):
        return lax.rem(sec + d, ns)

    def z_peer(d):
        return lax.rem(z + d, nz)

    def y_peer(d):
        return lax.rem(y + d, ny)

    t_offsets = [(dy, dc) for dy in range(ny) for dc in range(nc)]
    t_offsets.sort(key=lambda o: (min(o[0], ny - o[0]), o[1]))

    def t_peer(o):
        return lax.rem(y + o[0], ny), lax.rem(c + o[1], nc)

    barrier = pltpu.get_barrier_semaphore()
    count = 0
    for d in range(1, ns):
        pl.semaphore_signal(barrier, inc=1, device_id={"section": sec_peer(d), "seq": seq}, device_id_type=pl.DeviceIdType.MESH)
        count += 1
    for d in range(1, nz):
        pl.semaphore_signal(barrier, inc=1, device_id={"section": sec, "seq": seq_of(y, z_peer(d), c)}, device_id_type=pl.DeviceIdType.MESH)
        count += 1
    for o in t_offsets[1:]:
        y_, c_ = t_peer(o)
        pl.semaphore_signal(barrier, inc=1, device_id={"section": sec, "seq": seq_of(y_, z, c_)}, device_id_type=pl.DeviceIdType.MESH)
        count += 1
    pl.semaphore_wait(barrier, count)

    def first_copies():
        return [rcopy(w_ref.at[sec_peer(d)], W.at[sec, y, z, c], p1s.at[d - 1], p1r.at[sec], sec_peer(d), seq) for d in range(1, ns)]

    def first_wait(s):
        @pl.when(s != sec)
        def _():
            rcopy(w_ref.at[s], W.at[s, y, z, c], p1s.at[0], p1r.at[s], sec, seq).wait_recv()

    def z_copies(s):
        return [rcopy(W.at[s, y, z, c], W.at[s, y, z, c], zs.at[d - 1], zr.at[s, z], sec, seq_of(y, z_peer(d), c)) for d in range(1, nz)]

    def z_wait(s):
        for d in range(1, nz):
            p = z_peer(d)
            rcopy(W.at[s, y, p, c], W.at[s, y, p, c], zs.at[d - 1], zr.at[s, p], sec, seq).wait_recv()

    def y_copies(s):
        return [rcopy(W.at[s, y, :, c], W.at[s, y, :, c], ys.at[d - 1], yr.at[s, y], sec, seq_of(y_peer(d), z, c)) for d in range(1, ny)]

    def y_wait(s):
        for d in range(1, ny):
            p = y_peer(d)
            rcopy(W.at[s, p, :, c], W.at[s, p, :, c], ys.at[d - 1], yr.at[s, p], sec, seq).wait_recv()

    def c_copy(s):
        return rcopy(W.at[s, :, :, c], W.at[s, :, :, c], cs.at[0], cr.at[s], sec, seq_of(y, z, 1 - c))

    def c_wait(s):
        rcopy(W.at[s, :, :, 1 - c], W.at[s, :, :, 1 - c], cs.at[0], cr.at[s], sec, seq).wait_recv()

    def gather_copies(buf, ssem, rsem):
        return [rcopy(buf.at[sec], buf.at[sec], ssem.at[d - 1], rsem.at[sec], sec_peer(d), seq) for d in range(1, ns)]

    def gather_wait(buf, ssem, rsem):
        for d in range(1, ns):
            p = sec_peer(d)
            rcopy(buf.at[p], buf.at[p], ssem.at[d - 1], rsem.at[p], sec, seq).wait_recv()

    def kv_copies(par):
        out = []
        for i, o in enumerate(t_offsets[1:]):
            y_, c_ = t_peer(o)
            out.append(rcopy(KV.at[par, t], KV.at[par, t], kvs.at[i], kvr.at[par, t], sec, seq_of(y_, z, c_)))
        return out

    def start(copies):
        for copy in copies:
            copy.start()

    def wait_send(copies):
        for copy in copies:
            copy.wait_send()

    start(first_copies())
    W[sec, y, z, c] = w_ref[sec]
    lat_copies = [
        rcopy(lat_ref.at[z_peer(d)], H.at[sec, pl.ds(z * tok, tok)], os_.at[d - 1], or_.at[z], sec, seq_of(y, z_peer(d), c))
        for d in range(1, nz)
    ]
    start(lat_copies)
    H[sec, pl.ds(pl.multiple_of(z * tok, tok), tok), :] = lat_ref[z]
    first_wait(0)
    start(z_copies(0))
    for d in range(1, nz):
        p = z_peer(d)
        rcopy(lat_ref.at[p], H.at[sec, pl.ds(p * tok, tok)], os_.at[d - 1], or_.at[p], sec, seq).wait_recv()
    z_wait(0)
    start(y_copies(0))
    wait_send(z_copies(0))
    wait_send(lat_copies)
    for s in range(1, ns):
        first_wait(s)
    wait_send(first_copies())
    y_wait(0)
    wait_send(y_copies(0))
    c_copy(0).start()

    def weights(s, lo, hi):
        return W[s, :, :, :, :, lo:hi].reshape(dim, hi - lo)

    def whole(buf):
        return jnp.concatenate([buf[p] for p in range(ns)], axis=1)

    lane = lax.broadcasted_iota(jnp.int32, (rows, SLICE), 1)

    def block(s, decoder):
        par = lax.rem(s, 2)
        more = s + 1 < ns
        start(gather_copies(H, hs, hr))

        @pl.when(more)
        def _():
            start(z_copies(s + 1))

        c_wait(s)
        c_copy(s).wait_send()
        gather_wait(H, hs, hr)
        if decoder:
            @pl.when(s == ns // 2)
            def _():
                skips[s - 1] = jnp.dot(whole(H), weights(s - 1, 512, 640), preferred_element_type=F32).astype(BF16)

            merged = jnp.dot(whole(H), weights(s, 512, 640), preferred_element_type=F32)
            U[sec] = (merged + skips[ns - 1 - s].astype(F32)).astype(BF16)
            start(gather_copies(U, us, ur))
            gather_wait(U, us, ur)
            src = U
        else:
            src = H
        total = jnp.zeros((rows, SLICE), F32)
        for p in range(ns):
            total = total + src[p].astype(F32)
        mean = jnp.sum(total, axis=-1, keepdims=True) * (1.0 / dim)
        total = jnp.zeros((rows, SLICE), F32)
        for p in range(ns):
            center = src[p].astype(F32) - mean
            total = total + center * center
        spread = jnp.sum(total, axis=-1, keepdims=True) * (1.0 / dim)
        inverse = lax.rsqrt(spread + EPSILON)
        normed = jnp.concatenate([((src[p].astype(F32) - mean) * inverse).astype(BF16) for p in range(ns)], axis=1)
        kv = jnp.dot(normed, weights(s, 128, 384), preferred_element_type=F32)
        KV[par, t] = kv.astype(BF16)
        start(kv_copies(par))
        q = jnp.dot(normed, weights(s, 0, 128), preferred_element_type=F32)
        q_heads = [jnp.where(lane < HEAD_DIM, q, 0.0).astype(BF16), jnp.where(lane < HEAD_DIM, 0.0, q).astype(BF16)]

        @pl.when(more)
        def _():
            z_wait(s + 1)
            start(y_copies(s + 1))
            wait_send(z_copies(s + 1))

        if not decoder:
            @pl.when(s >= 1)
            def _():
                skips[s - 1] = jnp.dot(whole(H), weights(s - 1, 512, 640), preferred_element_type=F32).astype(BF16)

        wait_send(gather_copies(H, hs, hr))
        if decoder:
            wait_send(gather_copies(U, us, ur))

        tops = [None, None]
        for i, o in enumerate(t_offsets):
            y_, c_ = t_peer(o)
            slot = y_ * nc + c_
            if i > 0:
                rcopy(KV.at[par, slot], KV.at[par, slot], kvs.at[i - 1], kvr.at[par, slot], sec, seq).wait_recv()
            keys = KV[par, slot, :, 0:SLICE]
            for h in range(2):
                scores = lax.dot_general(q_heads[h], keys, (((1,), (1,)), ((), ())), preferred_element_type=F32)
                S[h, i] = scores
                top = jnp.max(scores, axis=-1, keepdims=True)
                tops[h] = top if tops[h] is None else jnp.maximum(tops[h], top)
        mixes = []
        for h in range(2):
            acc = jnp.zeros((rows, SLICE), F32)
            sums = jnp.zeros((rows, 1), F32)
            for i, o in enumerate(t_offsets):
                y_, c_ = t_peer(o)
                slot = y_ * nc + c_
                e = jnp.exp2(S[h, i] - tops[h])
                sums = sums + jnp.sum(e, axis=-1, keepdims=True)
                acc = acc + jnp.dot(e.astype(BF16), KV[par, slot, :, SLICE:2 * SLICE], preferred_element_type=F32)
            mixes.append(acc / sums)
        A[sec] = jnp.where(lane < HEAD_DIM, mixes[0], mixes[1]).astype(BF16)
        start(gather_copies(A, as_, ar))
        wait_send(kv_copies(par))

        @pl.when(more)
        def _():
            y_wait(s + 1)
            wait_send(y_copies(s + 1))
            c_copy(s + 1).start()

        gather_wait(A, as_, ar)
        update = jnp.dot(whole(A), weights(s, 384, 512), preferred_element_type=F32)
        H[sec] = (src[sec].astype(F32) + update).astype(BF16)
        wait_send(gather_copies(A, as_, ar))

    def encoder_step(s, carry):
        block(s, False)
        return carry

    def decoder_step(s, carry):
        block(s, True)
        return carry

    lax.fori_loop(0, ns // 2, encoder_step, 0)
    lax.fori_loop(ns // 2, ns, decoder_step, 0)

    out_copies = [
        rcopy(H.at[sec, pl.ds(z_peer(d) * tok, tok)], O.at[z], os_.at[d - 1], or_.at[z], sec, seq_of(y, z_peer(d), c))
        for d in range(1, nz)
    ]
    start(out_copies)
    O[z] = H[sec, pl.ds(pl.multiple_of(z * tok, tok), tok), :]
    for d in range(1, nz):
        p = z_peer(d)
        rcopy(O.at[p], O.at[p], os_.at[d - 1], or_.at[p], sec, seq).wait_recv()
    out_ref[...] = O[...]
    wait_send(out_copies)


def body(latents, norm_gain, qkv_weight, proj_weight, merge_weight):
    windows, tok, dim = latents.shape
    ns = lax.axis_size("section")
    nseq = lax.axis_size("seq")
    nz = windows
    ny = nseq // (nz * CORES)
    part = dim // nseq
    sec = lax.axis_index("section")
    seq = lax.axis_index("seq")
    rows = nz * tok
    nt = ny * CORES
    lat = lax.dynamic_slice_in_dim(latents, sec * SLICE, SLICE, axis=2)
    gain = lax.dynamic_slice_in_dim(norm_gain[0], seq * part, part)[:, None]
    scale = jnp.where(jnp.arange(3 * dim) < dim, HEAD_DIM ** (-0.5) * math.log2(math.e), 1.0).astype(F32)
    folded = (qkv_weight[0].astype(F32) * gain * scale[None, :]).astype(BF16)
    packed = jnp.concatenate([folded, proj_weight[0], merge_weight[0]], axis=1)
    packed = packed.reshape(part, 5, ns, SLICE).transpose(2, 0, 1, 3).reshape(ns, part, 5 * SLICE)
    dma = pltpu.SemaphoreType.DMA
    vmem = pl.BlockSpec(memory_space=pltpu.VMEM)
    return pl.pallas_call(
        functools.partial(kernel, ns, ny, nz, tok),
        out_shape=jax.ShapeDtypeStruct((nz, tok, SLICE), BF16),
        in_specs=[vmem, vmem],
        out_specs=vmem,
        scratch_shapes=[
            pltpu.VMEM((ns, rows, SLICE), BF16),
            pltpu.VMEM((ns, rows, SLICE), BF16),
            pltpu.VMEM((ns, rows, SLICE), BF16),
            pltpu.VMEM((2, nt, rows, 2 * SLICE), BF16),
            pltpu.VMEM((2, nt, rows, rows), F32),
            pltpu.VMEM((ns, ny, nz, CORES, part, 5 * SLICE), BF16),
            pltpu.VMEM((ns // 2, rows, SLICE), BF16),
            pltpu.VMEM((nz, tok, SLICE), BF16),
            dma((ns - 1,)), dma((ns,)),
            dma((nz - 1,)), dma((ns, nz)),
            dma((ny - 1,)), dma((ns, ny)),
            dma((1,)), dma((ns,)),
            dma((ns - 1,)), dma((ns,)),
            dma((ns - 1,)), dma((ns,)),
            dma((ns - 1,)), dma((ns,)),
            dma((nt - 1,)), dma((2, nt)),
            dma((nz - 1,)), dma((nz,)),
        ],
        compiler_params=pltpu.CompilerParams(collective_id=0, has_side_effects=True, vmem_limit_bytes=48 * 1024 * 1024),
        name="blocks",
    )(lat, packed)


def solution(mesh):
    placed = (
        P(None, "seq", None),
        P("section", None),
        P("section", "seq", None),
        P("section", "seq", None),
        P("section", "seq", None),
    )
    return jax.shard_map(
        body, mesh=mesh, in_specs=placed, out_specs=P(None, "seq", "section"), check_vma=False
    )
```

time: 1420 us -> 357 us (0.25)
  waiting for transfers between devices: 724 us -> 0 us
  starting transfers between devices: 458 us -> 0 us
  Pallas kernels: 0 us -> 348 us
  local copies, waits for them, and re-layouts: 95.2 us -> 2 us
  other arithmetic: 83.3 us -> 1.1 us
  matrix products: 40.5 us -> 0 us
    all_to_all x44 -> x0, waiting for transfers between devices: 383 us -> none  [the longest x11 112 us: tick(): lax.all_to_all(values_in, 'seq', split_axis=0, concat_axis=0, tiled=True)]
    pallas_call x0 -> x1, Pallas kernels: none -> 348 us  [body(): pl.pallas_call(functools.partial(kernel, ns, ny, nz, tok), out_shape=jax....]
    all_to_all x44 -> x0, starting transfers between devices: 249 us -> none  [the longest x11 68 us: tick(): lax.all_to_all(attended, 'seq', split_axis=0, concat_axis=0, tiled=True)]
    ppermute x44 -> x0, starting transfers between devices: 209 us -> none  [the longest x33 187 us: partner(): return lax.ppermute(value, axis, pairs)]
    all_gather x3 -> x0, waiting for transfers between devices: 182 us -> none  [the longest x1 69.7 us: body(): lax.all_gather(qkv_weight, 'seq', axis=1, tiled=True)]
    ppermute x44 -> x0, waiting for transfers between devices: 119 us -> none  [the longest x33 119 us: partner(): return lax.ppermute(value, axis, pairs)]
    while x126 -> x0, local copies, waits for them, and re-layouts: 46.6 us -> none
    dot_general x28 -> x0, matrix products: 40.5 us -> none  [the longest x4 16.3 us: project(): jnp.dot(normed, w_qkv, preferred_element_type=jnp.float32)]
  transfers between devices with their start and end apart: 92 -> 0, of which waited for: 81 -> 0; matrix products, arithmetic and copies ran while one was open for 5% -> 0% of each run, Pallas kernels for 0% -> 0%
where the time goes in v1:
time: 357 us; the launch traced here: 351 us
  Pallas kernels  348 us (97%)
    pallas_call x1, Pallas kernels, body(): pl.pallas_call(functools.partial(kernel, ns, ny, nz, tok), out_shape=jax....  348 us

profile of v1, /device:TPU:8, one launch (start us, length us, event | category | flops | bytes accessed | tf_op | source)
XLA Modules:
  0.0 351.2 jit_solution(9026309799817421867)
XLA Ops:
  0.0 0.0 copy-start
  0.0 0.8 dynamic-slice_bitcast_fusion
  0.8 0.0 copy-start.1
  0.8 0.0 copy-start.2
  0.8 1.1 fusion.1
  1.9 0.0 copy-done.1
  1.9 0.0 copy-done.2
  2.0 0.1 copy.10
  2.1 0.4 reshape.17.w_ref
  2.5 0.0 copy-done
  2.5 348.0 %blocks.1 = bf16[4,64,128]{2,1,0:T(8,128)(2,1)S(1)} custom-call(bf16[4,64,128]{2,1,0:T(8,128)(2,1)S(1)} %constant_dynamic-slice_fusion.lat_ref, bf16[8,32,640]{2,1,0:T(8,128)(2,1)S(1)} %reshape.17.w_ref), custom_call_target="tpu_custom_call" | custom-call | tf_op jit(solution)/shard_map/blocks/pallas_call | solution.py:297
  350.6 0.6 copy.12
  (4 shorter events, 0.1 us)
Async XLA Ops:
  0.0 2.5 copy-start
  0.8 1.1 copy-start.1
  0.8 1.1 copy-start.2

commit v2 on v1

v2 whole, which is shorter than its diff:
```python
import functools
import math

import jax
import jax.numpy as jnp
from jax import lax
from jax.experimental import pallas as pl
from jax.experimental.pallas import tpu as pltpu
from jax.sharding import PartitionSpec as P

HEAD_DIM = 64
SLICE = 128
CORES = 2
EPSILON = 1e-05
F32 = jnp.float32
BF16 = jnp.bfloat16
MESH = pl.DeviceIdType.MESH


def rcopy(src, dst, send, recv, section, seq):
    return pltpu.make_async_remote_copy(
        src_ref=src,
        dst_ref=dst,
        send_sem=send,
        recv_sem=recv,
        device_id={"section": section, "seq": seq},
        device_id_type=MESH,
    )


def start(copies):
    for copy in copies:
        copy.start()


def wait_send(copies):
    for copy in copies:
        copy.wait_send()


def wait_recv(copies):
    for copy in copies:
        copy.wait_recv()


def kernel(ns, ny, nz, tok, lat_ref, w_ref, m_ref, p_ref, out_ref,
           H, A, KV, S, R, W, MD, WP, skips, O,
           p1s, p1r, m1s, m1r, q1s, q1r, wzs, wzr, wys, wyr, wcs, wcr,
           mzs, mzr, mys, myr, mcs, mcr, hs, hr, as_, ar, kvs, kvr, rls, os_, or_):
    nc = CORES
    nt = ny * nc
    mid = ns // 2
    dim = ns * SLICE
    zh = nz // 2
    half = zh * tok
    sec = lax.axis_index("section")
    seq = lax.axis_index("seq")
    y = seq // (nz * nc)
    z = (seq // nc) % nz
    c = seq % nc
    t = y * nc + c

    def seq_of(y_, z_, c_):
        return y_ * (nz * nc) + z_ * nc + c_

    def sec_peer(d):
        return lax.rem(sec + d, ns)

    def z_peer(d):
        return lax.rem(z + d, nz)

    def y_peer(d):
        return lax.rem(y + d, ny)

    y_order = sorted(range(1, ny), key=lambda d: min(d, ny - d))
    sibling = seq_of(y, z, 1 - c)

    barrier = pltpu.get_barrier_semaphore()
    greeted = [(sec_peer(d), seq) for d in range(1, ns)]
    greeted += [(sec, seq_of(y, z_peer(d), c)) for d in range(1, nz)]
    greeted += [(sec, seq_of(y_peer(d), z, c)) for d in range(1, ny)]
    greeted += [(sec, sibling)]
    for section_, seq_ in greeted:
        pl.semaphore_signal(barrier, inc=1, device_id={"section": section_, "seq": seq_}, device_id_type=MESH)
    pl.semaphore_wait(barrier, len(greeted))

    def first_copies():
        out = []
        for d in range(1, ns):
            p = sec_peer(d)
            out.append(rcopy(w_ref.at[p], W.at[sec, y, z, c], p1s.at[d - 1], p1r.at[sec], p, seq))
            out.append(rcopy(m_ref.at[p], MD.at[sec % mid, y, z, c, sec // mid], m1s.at[d - 1], m1r.at[sec], p, seq))
        return out

    def first_wait(s):
        @pl.when(sec != s)
        def _():
            rcopy(w_ref.at[s], W.at[s, y, z, c], p1s.at[0], p1r.at[s], sec, seq).wait_recv()

    def merge_wait(s):
        @pl.when(sec != s)
        def _():
            rcopy(m_ref.at[s], MD.at[s % mid, y, z, c, s // mid], m1s.at[0], m1r.at[s], sec, seq).wait_recv()

    composed = (sec >= mid - 1) & (sec < ns - 1)

    def proj_copies():
        return [rcopy(p_ref, WP.at[sec - (mid - 1)], q1s.at[d - 1], q1r.at[sec - (mid - 1)], sec_peer(d), seq) for d in range(1, ns)]

    def proj_wait(i):
        @pl.when(sec != i + mid - 1)
        def _():
            rcopy(p_ref, WP.at[i], q1s.at[0], q1r.at[i], sec, seq).wait_recv()

    w_sems = (wzs, wzr, wys, wyr, wcs, wcr)
    m_sems = (mzs, mzr, mys, myr, mcs, mcr)

    def z_copies(ref, sems, s):
        return [rcopy(ref.at[s, y, z, c], ref.at[s, y, z, c], sems[0].at[d - 1], sems[1].at[s, z], sec, seq_of(y, z_peer(d), c)) for d in range(1, nz)]

    def z_waits(ref, sems, s):
        wait_recv([rcopy(ref.at[s, y, z_peer(d), c], ref.at[s, y, z_peer(d), c], sems[0].at[d - 1], sems[1].at[s, z_peer(d)], sec, seq) for d in range(1, nz)])

    def y_copies(ref, sems, s):
        return [rcopy(ref.at[s, y, :, c], ref.at[s, y, :, c], sems[2].at[d - 1], sems[3].at[s, y], sec, seq_of(y_peer(d), z, c)) for d in y_order]

    def y_waits(ref, sems, s):
        wait_recv([rcopy(ref.at[s, y_peer(d), :, c], ref.at[s, y_peer(d), :, c], sems[2].at[d - 1], sems[3].at[s, y_peer(d)], sec, seq) for d in y_order])

    def c_copy(ref, sems, s):
        return rcopy(ref.at[s, :, :, c], ref.at[s, :, :, c], sems[4].at[0], sems[5].at[s], sec, sibling)

    def c_wait(ref, sems, s):
        c_copy(ref, sems, s).wait_send()
        rcopy(ref.at[s, :, :, 1 - c], ref.at[s, :, :, 1 - c], sems[4].at[0], sems[5].at[s], sec, seq).wait_recv()

    def stage_z(ref, sems, s):
        start(z_copies(ref, sems, s))

    def stage_y(ref, sems, s):
        z_waits(ref, sems, s)
        start(y_copies(ref, sems, s))
        wait_send(z_copies(ref, sems, s))

    def stage_c(ref, sems, s):
        y_waits(ref, sems, s)
        c_copy(ref, sems, s).start()
        wait_send(y_copies(ref, sems, s))

    def prefetch(stage, s):
        @pl.when(s < ns - 1)
        def _():
            stage(W, w_sems, s + 1)

        @pl.when(s < mid)
        def _():
            stage(MD, m_sems, s)

    def gather_copies(buf, ssem, rsem, g):
        return [rcopy(buf.at[g, sec], buf.at[g, sec], ssem.at[g, d - 1], rsem.at[g, sec], sec_peer(d), seq) for d in range(1, ns)]

    def gather_wait(buf, ssem, rsem, g):
        wait_recv([rcopy(buf.at[g, sec_peer(d)], buf.at[g, sec_peer(d)], ssem.at[g, d - 1], rsem.at[g, sec_peer(d)], sec, seq) for d in range(1, ns)])

    def kv_copies(par, g):
        out = [rcopy(KV.at[par, g, t], KV.at[par, g, t], kvs.at[g, d], kvr.at[par, g, t], sec, seq_of(y_peer(d), z, c)) for d in y_order]
        out.append(rcopy(KV.at[par, g, t], KV.at[par, g, t], kvs.at[g, 0], kvr.at[par, g, t], sec, sibling))
        return out

    def kv_slot(d, dc):
        return y_peer(d) * nc + (c if dc == 0 else 1 - c)

    def kv_wait(par, g, d, dc):
        slot = kv_slot(d, dc)
        rcopy(KV.at[par, g, slot], KV.at[par, g, slot], kvs.at[g, 0], kvr.at[par, g, slot], sec, seq).wait_recv()

    def relay(par, g, d):
        slot = kv_slot(d, 0)
        return rcopy(KV.at[par, g, slot], KV.at[par, g, slot], rls.at[g, d], kvr.at[par, g, slot], sec, sibling)

    def rows_of(z_):
        return pl.ds(lax.rem(z_, zh) * tok, tok)

    def local_rows(z_):
        return pl.ds(pl.multiple_of(lax.rem(z_, zh) * tok, tok), tok)

    start(first_copies())
    lat_copies = [
        rcopy(lat_ref.at[z_peer(d)], H.at[z // zh, sec, rows_of(z)], os_.at[d - 1], or_.at[z], sec, seq_of(y, z_peer(d), c))
        for d in range(1, nz)
    ]
    start(lat_copies)
    W[sec, y, z, c] = w_ref[sec]
    MD[sec % mid, y, z, c, sec // mid] = m_ref[sec]
    H[z // zh, sec, local_rows(z), :] = lat_ref[z]

    @pl.when(composed)
    def _():
        start(proj_copies())
        WP[sec - (mid - 1)] = p_ref[...]

    first_wait(0)
    stage_z(W, w_sems, 0)
    for d in range(1, nz):
        p = z_peer(d)
        rcopy(lat_ref.at[p], H.at[p // zh, sec, rows_of(p)], os_.at[d - 1], or_.at[p], sec, seq).wait_recv()
    for g in range(2):
        start(gather_copies(H, hs, hr, g))
    stage_y(W, w_sems, 0)
    wait_send(lat_copies)
    for s in range(1, ns):
        first_wait(s)
    for s in range(ns):
        merge_wait(s)
    for i in range(mid):
        proj_wait(i)
    wait_send(first_copies())

    @pl.when(composed)
    def _():
        wait_send(proj_copies())

    MD[0, y, z, c, 1] = (MD[0, y, z, c, 1].astype(F32) + MD[mid - 1, y, z, c, 0].astype(F32)).astype(BF16)
    skips[mid - 1] = jnp.zeros((2, half, SLICE), BF16)
    stage_c(W, w_sems, 0)

    def weights(s, lo, hi):
        return W[s, :, :, :, :, lo:hi].reshape(dim, hi - lo)

    def merge_weights(s, which):
        return MD[s, :, :, :, which].reshape(dim, SLICE)

    def whole(buf, g):
        return jnp.concatenate([buf[g, p] for p in range(ns)], axis=1)

    lane = lax.broadcasted_iota(jnp.int32, (half, SLICE), 1)
    pairs = [((0, 0), (0, 1))]
    near = y_order[:-1] if len(y_order) > 1 else []
    if near:
        pairs += [((near[0], 0), (near[1], 0)), ((near[0], 1), (near[1], 1))]
    pairs += [((y_order[-1], 0), (y_order[-1], 1))]

    def block(s, carry):
        par = lax.rem(s, 2)
        c_wait(W, w_sems, s)

        @pl.when((s >= 1) & (s <= mid))
        def _():
            c_wait(MD, m_sems, s - 1)

        stacked = []
        for g in range(2):
            gather_wait(H, hs, hr, g)
            total = jnp.zeros((half, SLICE), F32)
            for p in range(ns):
                total = total + H[g, p].astype(F32)
            mean = jnp.sum(total, axis=-1, keepdims=True) * (1.0 / dim)
            total = jnp.zeros((half, SLICE), F32)
            for p in range(ns):
                center = H[g, p].astype(F32) - mean
                total = total + center * center
            spread = jnp.sum(total, axis=-1, keepdims=True) * (1.0 / dim)
            inverse = lax.rsqrt(spread + EPSILON)
            normed = jnp.concatenate([((H[g, p].astype(F32) - mean) * inverse).astype(BF16) for p in range(ns)], axis=1)
            kv = jnp.dot(normed, weights(s, 128, 384), preferred_element_type=F32)
            KV[par, g, t] = kv.astype(BF16)
            start(kv_copies(par, g))
            q = jnp.dot(normed, weights(s, 0, 128), preferred_element_type=F32)
            stacked.append(jnp.concatenate([jnp.where(lane < HEAD_DIM, q, 0.0), jnp.where(lane < HEAD_DIM, 0.0, q)], axis=0).astype(BF16))

        prefetch(stage_z, s)
        for g in range(2):
            @pl.when((s >= mid - 1) & (s < ns - 1))
            def _():
                merged = jnp.dot(whole(H, g), merge_weights(s - (mid - 1), 1), preferred_element_type=F32)
                R[g] = merged + skips[ns - 2 - s, g].astype(F32)

            @pl.when((s < mid - 1) | (s == ns - 1))
            def _():
                R[g] = H[g, sec].astype(F32)

            @pl.when((s >= 1) & (s < mid))
            def _():
                skips[s - 1, g] = jnp.dot(whole(H, g), merge_weights(s - 1, 0), preferred_element_type=F32).astype(BF16)

        @pl.when((s >= 1) & (s <= mid))
        def _():
            rows = jnp.dot(WP[s - 1], merge_weights(s - 1, 1), preferred_element_type=F32)
            W[s + mid - 2, y, z, c, :, 384:512] = rows.astype(BF16)

        tops = [None, None]
        for g in range(2):
            for i, pair in enumerate(pairs):
                for d, dc in pair:
                    if (d, dc) != (0, 0):
                        kv_wait(par, g, d, dc)
                        if dc == 0:
                            relay(par, g, d).start()

                keys = jnp.concatenate([KV[par, g, kv_slot(d, dc), :, 0:SLICE] for d, dc in pair], axis=0)
                for gq in range(2):
                    scores = lax.dot_general(stacked[gq], keys, (((1,), (1,)), ((), ())), preferred_element_type=F32)
                    S[gq, g, i] = scores
                    for lo in range(0, scores.shape[1], min(SLICE, scores.shape[1])):
                        part = scores[:, lo:lo + SLICE]
                        tops[gq] = part if tops[gq] is None else jnp.maximum(tops[gq], part)
        prefetch(stage_y, s)
        for g in range(2):
            wait_send(gather_copies(H, hs, hr, g))
        for gq in range(2):
            top = jnp.max(tops[gq], axis=-1, keepdims=True)
            acc = jnp.zeros((2 * half, SLICE), F32)
            sums = None
            for g in range(2):
                for i, pair in enumerate(pairs):
                    e = jnp.exp2(S[gq, g, i] - top)
                    for lo in range(0, e.shape[1], min(SLICE, e.shape[1])):
                        part = e[:, lo:lo + SLICE]
                        sums = part if sums is None else sums + part
                    vals = jnp.concatenate([KV[par, g, kv_slot(d, dc), :, SLICE:2 * SLICE] for d, dc in pair], axis=0)
                    acc = acc + jnp.dot(e.astype(BF16), vals, preferred_element_type=F32)
            mix = acc / jnp.sum(sums, axis=-1, keepdims=True)
            A[gq, sec] = jnp.where(lane < HEAD_DIM, mix[:half], mix[half:]).astype(BF16)
            start(gather_copies(A, as_, ar, gq))
        for g in range(2):
            wait_send(kv_copies(par, g))
            wait_send([relay(par, g, d) for d in y_order])
        for g in range(2):
            gather_wait(A, as_, ar, g)
            update = jnp.dot(whole(A, g), weights(s, 384, 512), preferred_element_type=F32)
            H[g, sec] = (R[g] + update).astype(BF16)

            @pl.when(s < ns - 1)
            def _():
                start(gather_copies(H, hs, hr, g))

        prefetch(stage_c, s)
        for g in range(2):
            wait_send(gather_copies(A, as_, ar, g))
        return carry

    lax.fori_loop(0, ns, block, 0)

    out_copies = [
        rcopy(H.at[z_peer(d) // zh, sec, rows_of(z_peer(d))], O.at[z], os_.at[d - 1], or_.at[z], sec, seq_of(y, z_peer(d), c))
        for d in range(1, nz)
    ]
    start(out_copies)
    O[z] = H[z // zh, sec, local_rows(z), :]
    wait_recv([rcopy(O.at[z_peer(d)], O.at[z_peer(d)], os_.at[d - 1], or_.at[z_peer(d)], sec, seq) for d in range(1, nz)])
    out_ref[...] = O[...]
    wait_send(out_copies)


def body(latents, norm_gain, qkv_weight, proj_weight, merge_weight):
    windows, tok, dim = latents.shape
    ns = lax.axis_size("section")
    nseq = lax.axis_size("seq")
    nz = windows
    ny = nseq // (nz * CORES)
    part = dim // nseq
    sec = lax.axis_index("section")
    seq = lax.axis_index("seq")
    half = nz * tok // 2
    nt = ny * CORES
    mid = ns // 2
    lat = lax.dynamic_slice_in_dim(latents, sec * SLICE, SLICE, axis=2)
    gain = lax.dynamic_slice_in_dim(norm_gain[0], seq * part, part)[:, None]
    scale = jnp.where(jnp.arange(3 * dim) < dim, HEAD_DIM ** (-0.5) * math.log2(math.e), 1.0).astype(F32)
    folded = (qkv_weight[0].astype(F32) * gain * scale[None, :]).astype(BF16)
    packed = jnp.concatenate([folded, proj_weight[0]], axis=1)
    packed = packed.reshape(part, 4, ns, SLICE).transpose(2, 0, 1, 3).reshape(ns, part, 4 * SLICE)
    merges = merge_weight[0].reshape(part, ns, SLICE).transpose(1, 0, 2)
    dma = pltpu.SemaphoreType.DMA
    vmem = pl.BlockSpec(memory_space=pltpu.VMEM)
    gather_sems = [dma((2, ns - 1)), dma((2, ns))]
    w_sems = [dma((nz - 1,)), dma((ns, nz)), dma((ny - 1,)), dma((ns, ny)), dma((1,)), dma((ns,))]
    return pl.pallas_call(
        functools.partial(kernel, ns, ny, nz, tok),
        out_shape=jax.ShapeDtypeStruct((nz, tok, SLICE), BF16),
        in_specs=[vmem] * 4,
        out_specs=vmem,
        scratch_shapes=[
            pltpu.VMEM((2, ns, half, SLICE), BF16),
            pltpu.VMEM((2, ns, half, SLICE), BF16),
            pltpu.VMEM((2, 2, nt, half, 2 * SLICE), BF16),
            pltpu.VMEM((2, 2, nt // 2, 2 * half, 2 * half), F32),
            pltpu.VMEM((2, half, SLICE), F32),
            pltpu.VMEM((ns, ny, nz, CORES, part, 4 * SLICE), BF16),
            pltpu.VMEM((mid, ny, nz, CORES, 2, part, SLICE), BF16),
            pltpu.VMEM((mid, part, dim), BF16),
            pltpu.VMEM((mid, 2, half, SLICE), BF16),
            pltpu.VMEM((nz, tok, SLICE), BF16),
            dma((ns - 1,)), dma((ns,)),
            dma((ns - 1,)), dma((ns,)),
            dma((ns - 1,)), dma((mid,)),
            *w_sems,
            *w_sems,
            *gather_sems,
            *gather_sems,
            dma((2, ny)), dma((2, 2, nt)), dma((2, ny)),
            dma((nz - 1,)), dma((nz,)),
        ],
        compiler_params=pltpu.CompilerParams(collective_id=0, has_side_effects=True, vmem_limit_bytes=48 * 1024 * 1024),
        name="blocks",
    )(lat, packed, merges, proj_weight[0])


def solution(mesh):
    placed = (
        P(None, "seq", None),
        P("section", None),
        P("section", "seq", None),
        P("section", "seq", None),
        P("section", "seq", None),
    )
    return jax.shard_map(
        body, mesh=mesh, in_specs=placed, out_specs=P(None, "seq", "section"), check_vma=False
    )
```

time: 357 us -> 240 us (0.67); the launches traced: 351 us -> 238 us
  Pallas kernels: 348 us -> 235 us
    pallas_call x1, Pallas kernels: 348 us -> 235 us  [body(): pl.pallas_call(functools.partial(kernel, ns, ny, nz, tok), out_shape=jax....]
where the time goes in v2:
time: 240 us; the launch traced here: 238 us
  Pallas kernels  235 us (98%)
  local copies, waits for them, and re-layouts  2.52 us (1%)
    pallas_call x1, Pallas kernels, body(): pl.pallas_call(functools.partial(kernel, ns, ny, nz, tok), out_shape=jax....  235 us

profile of v2, /device:TPU:8, one launch (start us, length us, event | category | flops | bytes accessed | tf_op | source)
XLA Modules:
  0.0 238.4 jit_solution(4674375284536497912)
XLA Ops:
  0.0 0.0 copy-start
  0.0 0.8 dynamic-slice_bitcast_fusion
  0.8 0.0 copy-start.1
  0.8 1.1 fusion.1
  1.9 0.0 copy-done.1
  2.0 0.1 copy.13
  2.1 0.1 reshape.17.w_ref
  2.2 0.0 copy-done
  2.2 0.0 copy-start.2
  2.2 0.8 copy-done.2
  3.1 234.7 %blocks.1 = bf16[4,64,128]{2,1,0:T(8,128)(2,1)S(1)} custom-call(bf16[4,64,128]{2,1,0:T(8,128)(2,1)S(1)} %constant_dynamic-slice_fusion.lat_ref, bf16[8,32,512]{2,1,0:T(8,128)(2,1)S(1)} %reshape.17.w_ref, bf16[8,32,128]{2,1,0:T(8,128)(2,1)S(1)} %bitcast.19, bf16[32,1024]{1,0:T(8,128)(2,1)S(1)} %bitcast.21), custom_call_target="tpu_custom_call" | custom-call | tf_op jit(solution)/shard_map/blocks/pallas_call | solution.py:378
  237.8 0.6 copy.16
  (6 shorter events, 0.1 us)
Async XLA Ops:
  0.0 2.2 copy-start
  0.8 1.1 copy-start.1
  2.2 0.8 copy-start.2

commit v3 on v2

v3 whole, which is shorter than its diff:
```python
import functools
import math

import jax
import jax.numpy as jnp
from jax import lax
from jax.experimental import pallas as pl
from jax.experimental.pallas import tpu as pltpu
from jax.sharding import PartitionSpec as P

HEAD_DIM = 64
SLICE = 128
CORES = 2
EPSILON = 1e-05
F32 = jnp.float32
BF16 = jnp.bfloat16
MESH = pl.DeviceIdType.MESH


def rcopy(src, dst, send, recv, section, seq):
    return pltpu.make_async_remote_copy(
        src_ref=src,
        dst_ref=dst,
        send_sem=send,
        recv_sem=recv,
        device_id={"section": section, "seq": seq},
        device_id_type=MESH,
    )


def start(copies):
    for copy in copies:
        copy.start()


def wait_send(copies):
    for copy in copies:
        copy.wait_send()


def wait_recv(copies):
    for copy in copies:
        copy.wait_recv()


def kernel(ns, ny, nz, tok, lat_ref, w_ref, m_ref, p_ref, out_ref,
           H, A, KV, R, W, MD, WP, skips, O,
           p1s, p1r, m1s, m1r, q1s, q1r, wzs, wzr, wys, wyr, wcs, wcr,
           mzs, mzr, mys, myr, mcs, mcr, hs, hr, as_, ar, kvs, kvr, kvx, rls, os_, or_):
    nc = CORES
    mid = ns // 2
    dim = ns * SLICE
    zh = nz // 2
    half = zh * tok
    sec = lax.axis_index("section")
    seq = lax.axis_index("seq")
    y = seq // (nz * nc)
    z = (seq // nc) % nz
    c = seq % nc

    def seq_of(y_, z_, c_):
        return y_ * (nz * nc) + z_ * nc + c_

    nx = ns // 2
    farthest = [(dx, dz) for dx in range(nx) for dz in range(2) if (dx, dz) != (0, 0)]
    farthest.sort(key=lambda o: -(min(o[0], nx - o[0]) + o[1]))

    def sec_peer(d):
        dx, dz = farthest[d - 1]
        return lax.rem(sec // nx + dz, 2) * nx + lax.rem(sec + dx, nx)

    def z_peer(d):
        return lax.rem(z + d, nz)

    def y_peer(d):
        return lax.rem(y + d, ny)

    y_order = sorted(range(1, ny), key=lambda d: -min(d, ny - d))
    sibling = seq_of(y, z, 1 - c)

    barrier = pltpu.get_barrier_semaphore()
    greeted = [(sec_peer(d), seq) for d in range(1, ns)]
    greeted += [(sec, seq_of(y, z_peer(d), c)) for d in range(1, nz)]
    greeted += [(sec, seq_of(y_peer(d), z, c)) for d in range(1, ny)]
    greeted += [(sec, sibling)]
    for section_, seq_ in greeted:
        pl.semaphore_signal(barrier, inc=1, device_id={"section": section_, "seq": seq_}, device_id_type=MESH)
    pl.semaphore_wait(barrier, len(greeted))

    def first_copies():
        return [rcopy(w_ref.at[sec_peer(d)], W.at[sec, y, z, c], p1s.at[d - 1], p1r.at[sec], sec_peer(d), seq) for d in range(1, ns)]

    def merge_copies():
        return [
            rcopy(m_ref.at[sec_peer(d)], MD.at[sec % mid, y, z, c, sec // mid], m1s.at[d - 1], m1r.at[sec], sec_peer(d), seq)
            for d in range(1, ns)
        ]

    def first_wait(s):
        @pl.when(sec != s)
        def _():
            rcopy(w_ref.at[s], W.at[s, y, z, c], p1s.at[0], p1r.at[s], sec, seq).wait_recv()

    def merge_wait(s):
        @pl.when(sec != s)
        def _():
            rcopy(m_ref.at[s], MD.at[s % mid, y, z, c, s // mid], m1s.at[0], m1r.at[s], sec, seq).wait_recv()

    composed = (sec >= mid - 1) & (sec < ns - 1)

    def proj_copies():
        return [rcopy(p_ref, WP.at[sec - (mid - 1)], q1s.at[d - 1], q1r.at[sec - (mid - 1)], sec_peer(d), seq) for d in range(1, ns)]

    def proj_wait(i):
        @pl.when(sec != i + mid - 1)
        def _():
            rcopy(p_ref, WP.at[i], q1s.at[0], q1r.at[i], sec, seq).wait_recv()

    w_sems = (wzs, wzr, wys, wyr, wcs, wcr)
    m_sems = (mzs, mzr, mys, myr, mcs, mcr)

    def z_copies(ref, sems, s):
        return [rcopy(ref.at[s, y, z, c], ref.at[s, y, z, c], sems[0].at[0], sems[1].at[s], sec, seq_of(y, z_peer(d), c)) for d in range(1, nz)]

    def z_all(ref, sems, s):
        part = ref.at[s, y, pl.ds(0, nz - 1), c]
        return rcopy(part, part, sems[0].at[0], sems[1].at[s], sec, sibling)

    def y_copies(ref, sems, s):
        return [rcopy(ref.at[s, y, :, c], ref.at[s, y, :, c], sems[2].at[0], sems[3].at[s], sec, seq_of(y_peer(d), z, c)) for d in y_order]

    def y_all(ref, sems, s):
        part = ref.at[s, pl.ds(0, ny - 1), :, c]
        return rcopy(part, part, sems[2].at[0], sems[3].at[s], sec, sibling)

    def c_copy(ref, sems, s):
        return rcopy(ref.at[s, :, :, c], ref.at[s, :, :, c], sems[4].at[0], sems[5].at[s], sec, sibling)

    def c_wait(ref, sems, s):
        c_copy(ref, sems, s).wait_send()
        rcopy(ref.at[s, :, :, 1 - c], ref.at[s, :, :, 1 - c], sems[4].at[0], sems[5].at[s], sec, seq).wait_recv()

    def stage_z(ref, sems, s):
        start(z_copies(ref, sems, s))

    def stage_y(ref, sems, s):
        z_all(ref, sems, s).wait_recv()
        start(y_copies(ref, sems, s))
        z_all(ref, sems, s).wait_send()

    def stage_c(ref, sems, s):
        y_all(ref, sems, s).wait_recv()
        c_copy(ref, sems, s).start()
        y_all(ref, sems, s).wait_send()

    def prefetch(stage, s):
        @pl.when(s < ns - 1)
        def _():
            stage(W, w_sems, s + 1)

        @pl.when(s < mid)
        def _():
            stage(MD, m_sems, s)

    def gather_start(buf, ssem, rsem, g):
        start([rcopy(buf.at[g, sec], buf.at[g, sec], ssem.at[g], rsem.at[g], sec_peer(d), seq) for d in range(1, ns)])

    def gather_all(buf, ssem, rsem, g):
        part = buf.at[g, pl.ds(0, ns - 1)]
        return rcopy(part, part, ssem.at[g], rsem.at[g], sec, sibling)

    def kv_start(par, g):
        own = KV.at[par, g, c, y]
        start([rcopy(own, own, kvs.at[g], kvr.at[par, g, y], sec, seq_of(y_peer(d), z, c)) for d in y_order])
        rcopy(own, own, kvs.at[g], kvx.at[par, g], sec, sibling).start()

    def kv_sent(par, g):
        part = KV.at[par, g, c, pl.ds(0, ny)]
        rcopy(part, part, kvs.at[g], kvx.at[par, g], sec, sibling).wait_send()
        part = KV.at[par, g, c, pl.ds(0, ny - 1)]
        rcopy(part, part, rls.at[g], kvx.at[par, g], sec, sibling).wait_send()

    def kv_relay(par, g, d):
        p = y_peer(d)
        slot = KV.at[par, g, c, p]
        rcopy(slot, slot, rls.at[g], kvr.at[par, g, p], sec, sibling).wait_recv()
        rcopy(slot, slot, rls.at[g], kvx.at[par, g], sec, sibling).start()

    def kv_other(par, g):
        part = KV.at[par, g, 1 - c, pl.ds(0, ny)]
        rcopy(part, part, kvs.at[g], kvx.at[par, g], sec, sibling).wait_recv()

    def rows_of(z_):
        return pl.ds(lax.rem(z_, zh) * tok, tok)

    def local_rows(z_):
        return pl.ds(pl.multiple_of(lax.rem(z_, zh) * tok, tok), tok)

    @pl.when(sec == 0)
    def _():
        start(first_copies())

    lat_copies = [
        rcopy(lat_ref.at[z_peer(d)], H.at[z // zh, sec, rows_of(z)], os_.at[d - 1], or_.at[z], sec, seq_of(y, z_peer(d), c))
        for d in range(1, nz)
    ]
    start(lat_copies)
    W[sec, y, z, c] = w_ref[sec]
    MD[sec % mid, y, z, c, sec // mid] = m_ref[sec]
    H[z // zh, sec, local_rows(z), :] = lat_ref[z]

    @pl.when(composed)
    def _():
        WP[sec - (mid - 1)] = p_ref[...]

    first_wait(0)
    stage_z(W, w_sems, 0)
    for d in range(1, nz):
        p = z_peer(d)
        rcopy(lat_ref.at[p], H.at[p // zh, sec, rows_of(p)], os_.at[d - 1], or_.at[p], sec, seq).wait_recv()
    for g in range(2):
        gather_start(H, hs, hr, g)
    stage_y(W, w_sems, 0)

    @pl.when(sec != 0)
    def _():
        start(first_copies())

    start(merge_copies())
    wait_send(lat_copies)
    skips[mid - 1] = jnp.zeros((2, half, SLICE), BF16)
    stage_c(W, w_sems, 0)

    @pl.when(composed)
    def _():
        start(proj_copies())

    for s in range(1, ns):
        first_wait(s)
    for s in range(ns):
        merge_wait(s)
    wait_send(first_copies())
    wait_send(merge_copies())
    MD[0, y, z, c, 1] = (MD[0, y, z, c, 1].astype(F32) + MD[mid - 1, y, z, c, 0].astype(F32)).astype(BF16)

    def weights(s, lo, hi):
        return W[s, :, :, :, :, lo:hi].reshape(dim, hi - lo)

    def merge_weights(s, which):
        return MD[s, :, :, :, which].reshape(dim, SLICE)

    def whole(buf, g):
        return jnp.concatenate([buf[g, p] for p in range(ns)], axis=1)

    lane = lax.broadcasted_iota(jnp.int32, (half, SLICE), 1)
    def block(s, carry):
        par = lax.rem(s, 2)
        c_wait(W, w_sems, s)

        @pl.when((s >= 1) & (s <= mid))
        def _():
            c_wait(MD, m_sems, s - 1)

        stacked = []
        for g in range(2):
            gather_all(H, hs, hr, g).wait_recv()
            total = jnp.zeros((half, SLICE), F32)
            for p in range(ns):
                total = total + H[g, p].astype(F32)
            mean = jnp.sum(total, axis=-1, keepdims=True) * (1.0 / dim)
            total = jnp.zeros((half, SLICE), F32)
            for p in range(ns):
                center = H[g, p].astype(F32) - mean
                total = total + center * center
            spread = jnp.sum(total, axis=-1, keepdims=True) * (1.0 / dim)
            inverse = lax.rsqrt(spread + EPSILON)
            normed = jnp.concatenate([((H[g, p].astype(F32) - mean) * inverse).astype(BF16) for p in range(ns)], axis=1)
            kv = jnp.dot(normed, weights(s, 128, 384), preferred_element_type=F32)
            KV[par, g, c, y] = kv.astype(BF16)
            kv_start(par, g)
            q = jnp.dot(normed, weights(s, 0, 128), preferred_element_type=F32)
            stacked.append(jnp.concatenate([jnp.where(lane < HEAD_DIM, q, 0.0), jnp.where(lane < HEAD_DIM, 0.0, q)], axis=0).astype(BF16))

        prefetch(stage_z, s)
        for g in range(2):
            @pl.when((s >= mid - 1) & (s < ns - 1))
            def _():
                merged = jnp.dot(whole(H, g), merge_weights(s - (mid - 1), 1), preferred_element_type=F32)
                R[g] = merged + skips[ns - 2 - s, g].astype(F32)

            @pl.when((s < mid - 1) | (s == ns - 1))
            def _():
                R[g] = H[g, sec].astype(F32)

            @pl.when((s >= 1) & (s < mid))
            def _():
                skips[s - 1, g] = jnp.dot(whole(H, g), merge_weights(s - 1, 0), preferred_element_type=F32).astype(BF16)

        @pl.when((s >= 1) & (s <= mid))
        def _():
            rows = jnp.dot(WP[s - 1], merge_weights(s - 1, 1), preferred_element_type=F32)
            W[s + mid - 2, y, z, c, :, 384:512] = rows.astype(BF16)

        tops, sums, mixes = [None, None], [None, None], [None, None]

        def attend(gq, g, core):
            keys = KV[par, g, core, :, :, 0:SLICE].reshape(ny * half, SLICE)
            vals = KV[par, g, core, :, :, SLICE:2 * SLICE].reshape(ny * half, SLICE)
            scores = lax.dot_general(stacked[gq], keys, (((1,), (1,)), ((), ())), preferred_element_type=F32)
            top = jnp.max(scores, axis=-1, keepdims=True)
            if tops[gq] is not None:
                top = jnp.maximum(tops[gq], top)
            e = jnp.exp2(scores - top)
            mix = jnp.dot(e.astype(BF16), vals, preferred_element_type=F32)
            total = jnp.sum(e, axis=-1, keepdims=True)
            if tops[gq] is not None:
                fade = jnp.exp2(tops[gq] - top)
                mix = mixes[gq] * fade + mix
                total = sums[gq] * fade + total
            tops[gq], sums[gq], mixes[gq] = top, total, mix

        for g in range(2):
            for d in reversed(y_order):
                kv_relay(par, g, d)
            for gq in range(2):
                attend(gq, g, c)
            if g == 1:
                prefetch(stage_y, s)
                for half_ in range(2):
                    gather_all(H, hs, hr, half_).wait_send()
            kv_other(par, g)
            for gq in range(2):
                attend(gq, g, 1 - c)
                if g == 1:
                    mix = mixes[gq] / sums[gq]
                    A[gq, sec] = jnp.where(lane < HEAD_DIM, mix[:half], mix[half:]).astype(BF16)
                    gather_start(A, as_, ar, gq)
        for g in range(2):
            kv_sent(par, g)

        @pl.when(s == 0)
        def _():
            for i in range(mid):
                proj_wait(i)

        @pl.when((s == 0) & composed)
        def _():
            wait_send(proj_copies())

        for g in range(2):
            gather_all(A, as_, ar, g).wait_recv()
            update = jnp.dot(whole(A, g), weights(s, 384, 512), preferred_element_type=F32)
            H[g, sec] = (R[g] + update).astype(BF16)

            @pl.when(s < ns - 1)
            def _():
                gather_start(H, hs, hr, g)

        prefetch(stage_c, s)
        for g in range(2):
            gather_all(A, as_, ar, g).wait_send()
        return carry

    lax.fori_loop(0, ns, block, 0)

    out_copies = [
        rcopy(H.at[z_peer(d) // zh, sec, rows_of(z_peer(d))], O.at[z], os_.at[d - 1], or_.at[z], sec, seq_of(y, z_peer(d), c))
        for d in range(1, nz)
    ]
    start(out_copies)
    O[z] = H[z // zh, sec, local_rows(z), :]
    wait_recv([rcopy(O.at[z_peer(d)], O.at[z_peer(d)], os_.at[d - 1], or_.at[z_peer(d)], sec, seq) for d in range(1, nz)])
    out_ref[...] = O[...]
    wait_send(out_copies)


def body(latents, norm_gain, qkv_weight, proj_weight, merge_weight):
    windows, tok, dim = latents.shape
    ns = lax.axis_size("section")
    nseq = lax.axis_size("seq")
    nz = windows
    ny = nseq // (nz * CORES)
    part = dim // nseq
    sec = lax.axis_index("section")
    seq = lax.axis_index("seq")
    half = nz * tok // 2
    mid = ns // 2
    lat = lax.dynamic_slice_in_dim(latents, sec * SLICE, SLICE, axis=2)
    gain = lax.dynamic_slice_in_dim(norm_gain[0], seq * part, part)[:, None]
    scale = jnp.where(jnp.arange(3 * dim) < dim, HEAD_DIM ** (-0.5) * math.log2(math.e), 1.0).astype(F32)
    folded = (qkv_weight[0].astype(F32) * gain * scale[None, :]).astype(BF16)
    packed = jnp.concatenate([folded, proj_weight[0]], axis=1)
    packed = packed.reshape(part, 4, ns, SLICE).transpose(2, 0, 1, 3).reshape(ns, part, 4 * SLICE)
    merges = merge_weight[0].reshape(part, ns, SLICE).transpose(1, 0, 2)
    dma = pltpu.SemaphoreType.DMA
    vmem = pl.BlockSpec(memory_space=pltpu.VMEM)
    gather_sems = [dma((2,)), dma((2,))]
    w_sems = [dma((1,)), dma((ns,)), dma((1,)), dma((ns,)), dma((1,)), dma((ns,))]
    return pl.pallas_call(
        functools.partial(kernel, ns, ny, nz, tok),
        out_shape=jax.ShapeDtypeStruct((nz, tok, SLICE), BF16),
        in_specs=[vmem] * 4,
        out_specs=vmem,
        scratch_shapes=[
            pltpu.VMEM((2, ns, half, SLICE), BF16),
            pltpu.VMEM((2, ns, half, SLICE), BF16),
            pltpu.VMEM((2, 2, CORES, ny, half, 2 * SLICE), BF16),
            pltpu.VMEM((2, half, SLICE), F32),
            pltpu.VMEM((ns, ny, nz, CORES, part, 4 * SLICE), BF16),
            pltpu.VMEM((mid, ny, nz, CORES, 2, part, SLICE), BF16),
            pltpu.VMEM((mid, part, dim), BF16),
            pltpu.VMEM((mid, 2, half, SLICE), BF16),
            pltpu.VMEM((nz, tok, SLICE), BF16),
            dma((ns - 1,)), dma((ns,)),
            dma((ns - 1,)), dma((ns,)),
            dma((ns - 1,)), dma((mid,)),
            *w_sems,
            *w_sems,
            *gather_sems,
            *gather_sems,
            dma((2,)), dma((2, 2, ny)), dma((2, 2)), dma((2,)),
            dma((nz - 1,)), dma((nz,)),
        ],
        compiler_params=pltpu.CompilerParams(collective_id=0, has_side_effects=True, vmem_limit_bytes=48 * 1024 * 1024),
        name="blocks",
    )(lat, packed, merges, proj_weight[0])


def solution(mesh):
    placed = (
        P(None, "seq", None),
        P("section", None),
        P("section", "seq", None),
        P("section", "seq", None),
        P("section", "seq", None),
    )
    return jax.shard_map(
        body, mesh=mesh, in_specs=placed, out_specs=P(None, "seq", "section"), check_vma=False
    )
```

time: 240 us -> 211 us (0.88)
  Pallas kernels: 235 us -> 207 us
    pallas_call x1, Pallas kernels: 235 us -> 207 us  [body(): pl.pallas_call(functools.partial(kernel, ns, ny, nz, tok), out_shape=jax....]
where the time goes in v3:
time: 211 us
  Pallas kernels  207 us (98%)
  local copies, waits for them, and re-layouts  2.52 us (1%)
    pallas_call x1, Pallas kernels, body(): pl.pallas_call(functools.partial(kernel, ns, ny, nz, tok), out_shape=jax....  207 us

profile of v3, /device:TPU:8, one launch (start us, length us, event | category | flops | bytes accessed | tf_op | source)
XLA Modules:
  0.0 210.5 jit_solution(86125634191346744)
XLA Ops:
  0.0 0.0 copy-start
  0.0 0.8 dynamic-slice_bitcast_fusion
  0.8 0.0 copy-start.1
  0.8 1.1 fusion.1
  1.9 0.0 copy-done.1
  2.0 0.1 copy.13
  2.1 0.1 reshape.17.w_ref
  2.2 0.0 copy-done
  2.2 0.0 copy-start.2
  2.2 0.8 copy-done.2
  3.1 206.8 %blocks.1 = bf16[4,64,128]{2,1,0:T(8,128)(2,1)S(1)} custom-call(bf16[4,64,128]{2,1,0:T(8,128)(2,1)S(1)} %constant_dynamic-slice_fusion.lat_ref, bf16[8,32,512]{2,1,0:T(8,128)(2,1)S(1)} %reshape.17.w_ref, bf16[8,32,128]{2,1,0:T(8,128)(2,1)S(1)} %bitcast.19, bf16[32,1024]{1,0:T(8,128)(2,1)S(1)} %bitcast.21), custom_call_target="tpu_custom_call" | custom-call | tf_op jit(solution)/shard_map/blocks/pallas_call | solution.py:399
  209.9 0.6 copy.16
  (6 shorter events, 0.1 us)
Async XLA Ops:
  0.0 2.2 %copy-start = (bf16[4,64,1024]{2,1,0:T(8,128)(2,1)S(1)}, bf16[4,64,1024]{2,1,0:T(8,128)(2,1)}, u32[]{:S(2)}) copy-start(bf16[4,64,1024]{2,1,0:T(8,128)(2,1)} %param.5) | copy-start | bytes 1572868
  0.8 1.1 copy-start.1
  2.2 0.8 copy-start.2

commit v4 on v3

--- a/solution.py
+++ b/solution.py
@@ -43,9 +43,9 @@
         copy.wait_recv()
 
 
-def kernel(ns, ny, nz, tok, lat_ref, w_ref, m_ref, p_ref, out_ref,
-           H, A, KV, R, W, MD, WP, skips, O,
-           p1s, p1r, m1s, m1r, q1s, q1r, wzs, wzr, wys, wyr, wcs, wcr,
+def kernel(ns, ny, nz, tok, lat_hbm, gain_hbm, qkv_hbm, p_hbm, merge_hbm, out_ref,
+           lat_ref, gain_ref, qkv_ref, p_ref, merge_ref, in_sems, w_ref, m_ref, H, A, KV, R, W, MD, WP, skips, O,
+           p1s, p1r, m1s, m1r, q1s, q1r, z0r, wzs, wzr, wys, wyr, wcs, wcr,
            mzs, mzr, mys, myr, mcs, mcr, hs, hr, as_, ar, kvs, kvr, kvx, rls, os_, or_):
     nc = CORES
     mid = ns // 2
@@ -78,6 +78,13 @@
     y_order = sorted(range(1, ny), key=lambda d: -min(d, ny - d))
     sibling = seq_of(y, z, 1 - c)
 
+    columns = pl.ds(pl.multiple_of(sec * SLICE, SLICE), SLICE)
+    loads = [
+        pltpu.make_async_copy(src, dst, in_sems.at[i])
+        for i, (src, dst) in enumerate([
+            (qkv_hbm, qkv_ref), (gain_hbm, gain_ref), (p_hbm, p_ref), (merge_hbm, merge_ref), (lat_hbm.at[:, :, columns], lat_ref)])
+    ]
+    start(loads)
     barrier = pltpu.get_barrier_semaphore()
     greeted = [(sec_peer(d), seq) for d in range(1, ns)]
     greeted += [(sec, seq_of(y, z_peer(d), c)) for d in range(1, nz)]
@@ -85,6 +92,21 @@
     greeted += [(sec, sibling)]
     for section_, seq_ in greeted:
         pl.semaphore_signal(barrier, inc=1, device_id={"section": section_, "seq": seq_}, device_id_type=MESH)
+
+    for load in loads:
+        load.wait()
+    part = qkv_ref.shape[0]
+    places = lax.broadcasted_iota(jnp.int32, (part, dim), 1) - lax.broadcasted_iota(jnp.int32, (part, dim), 0)
+    gain = jnp.sum(jnp.where(places == seq * part, gain_ref[...], 0.0), axis=-1, keepdims=True)
+    for j in range(ns):
+        for k in range(3):
+            at = k * dim + j * SLICE
+            piece = qkv_ref[:, at:at + SLICE].astype(F32) * gain
+            if k == 0:
+                piece = piece * (HEAD_DIM ** (-0.5) * math.log2(math.e))
+            w_ref[j, :, k * SLICE:(k + 1) * SLICE] = piece.astype(BF16)
+        w_ref[j, :, 3 * SLICE:] = p_ref[:, j * SLICE:(j + 1) * SLICE]
+        m_ref[j] = merge_ref[:, j * SLICE:(j + 1) * SLICE]
     pl.semaphore_wait(barrier, len(greeted))
 
     def first_copies():
@@ -161,6 +183,30 @@
         @pl.when(s < mid)
         def _():
             stage(MD, m_sems, s)
+
+    def prefetch_z(s):
+        @pl.when(s < ns - 1)
+        def _():
+            @pl.when((s + 1 < mid - 1) | (s + 1 == ns - 1))
+            def _():
+                first_wait(s + 1)
+
+            stage_z(W, w_sems, s + 1)
+
+        @pl.when(s < mid)
+        def _():
+            @pl.when(s < mid - 1)
+            def _():
+                merge_wait(s)
+
+            merge_wait(s + mid)
+
+            @pl.when(s == 0)
+            def _():
+                merge_wait(mid - 1)
+                MD[0, y, z, c, 1] = (MD[0, y, z, c, 1].astype(F32) + MD[mid - 1, y, z, c, 0].astype(F32)).astype(BF16)
+
+            stage_z(MD, m_sems, s)
 
     def gather_start(buf, ssem, rsem, g):
         start([rcopy(buf.at[g, sec], buf.at[g, sec], ssem.at[g], rsem.at[g], sec_peer(d), seq) for d in range(1, ns)])
@@ -214,34 +260,31 @@
         WP[sec - (mid - 1)] = p_ref[...]
 
     first_wait(0)
-    stage_z(W, w_sems, 0)
+
+    def along_y(z_):
+        return [rcopy(W.at[0, y, z_, c], W.at[0, y, z_, c], wys.at[0], wyr.at[0], sec, seq_of(y_peer(d), z, c)) for d in y_order]
+
+    start([rcopy(W.at[0, y, z, c], W.at[0, y, z, c], wzs.at[0], z0r.at[z], sec, seq_of(y, z_peer(d), c)) for d in range(1, nz)])
+    start(along_y(z))
     for d in range(1, nz):
         p = z_peer(d)
         rcopy(lat_ref.at[p], H.at[p // zh, sec, rows_of(p)], os_.at[d - 1], or_.at[p], sec, seq).wait_recv()
-    for g in range(2):
-        gather_start(H, hs, hr, g)
-    stage_y(W, w_sems, 0)
+    gather_start(H, hs, hr, 0)
+    for d in sorted(range(1, nz), key=lambda d: min(d, nz - d)):
+        p = z_peer(d)
+        rcopy(W.at[0, y, p, c], W.at[0, y, p, c], wzs.at[0], z0r.at[p], sec, seq).wait_recv()
+        start(along_y(p))
+    gather_start(H, hs, hr, 1)
 
     @pl.when(sec != 0)
     def _():
         start(first_copies())
 
     start(merge_copies())
+    z_all(W, w_sems, 0).wait_send()
     wait_send(lat_copies)
     skips[mid - 1] = jnp.zeros((2, half, SLICE), BF16)
     stage_c(W, w_sems, 0)
-
-    @pl.when(composed)
-    def _():
-        start(proj_copies())
-
-    for s in range(1, ns):
-        first_wait(s)
-    for s in range(ns):
-        merge_wait(s)
-    wait_send(first_copies())
-    wait_send(merge_copies())
-    MD[0, y, z, c, 1] = (MD[0, y, z, c, 1].astype(F32) + MD[mid - 1, y, z, c, 0].astype(F32)).astype(BF16)
 
     def weights(s, lo, hi):
         return W[s, :, :, :, :, lo:hi].reshape(dim, hi - lo)
@@ -281,7 +324,12 @@
             q = jnp.dot(normed, weights(s, 0, 128), preferred_element_type=F32)
             stacked.append(jnp.concatenate([jnp.where(lane < HEAD_DIM, q, 0.0), jnp.where(lane < HEAD_DIM, 0.0, q)], axis=0).astype(BF16))
 
-        prefetch(stage_z, s)
+        prefetch_z(s)
+
+        @pl.when((s == 0) & composed)
+        def _():
+            start(proj_copies())
+
         for g in range(2):
             @pl.when((s >= mid - 1) & (s < ns - 1))
             def _():
@@ -296,8 +344,18 @@
             def _():
                 skips[s - 1, g] = jnp.dot(whole(H, g), merge_weights(s - 1, 0), preferred_element_type=F32).astype(BF16)
 
+        @pl.when(s == 1)
+        def _():
+            for i in range(mid):
+                proj_wait(i)
+
+            @pl.when(composed)
+            def _():
+                wait_send(proj_copies())
+
         @pl.when((s >= 1) & (s <= mid))
         def _():
+            first_wait(s + mid - 2)
             rows = jnp.dot(WP[s - 1], merge_weights(s - 1, 1), preferred_element_type=F32)
             W[s + mid - 2, y, z, c, :, 384:512] = rows.astype(BF16)
 
@@ -338,15 +396,6 @@
         for g in range(2):
             kv_sent(par, g)
 
-        @pl.when(s == 0)
-        def _():
-            for i in range(mid):
-                proj_wait(i)
-
-        @pl.when((s == 0) & composed)
-        def _():
-            wait_send(proj_copies())
-
         for g in range(2):
             gather_all(A, as_, ar, g).wait_recv()
             update = jnp.dot(whole(A, g), weights(s, 384, 512), preferred_element_type=F32)
@@ -371,6 +420,8 @@
     O[z] = H[z // zh, sec, local_rows(z), :]
     wait_recv([rcopy(O.at[z_peer(d)], O.at[z_peer(d)], os_.at[d - 1], or_.at[z_peer(d)], sec, seq) for d in range(1, nz)])
     out_ref[...] = O[...]
+    wait_send(first_copies())
+    wait_send(merge_copies())
     wait_send(out_copies)
 
 
@@ -381,17 +432,8 @@
     nz = windows
     ny = nseq // (nz * CORES)
     part = dim // nseq
-    sec = lax.axis_index("section")
-    seq = lax.axis_index("seq")
     half = nz * tok // 2
     mid = ns // 2
-    lat = lax.dynamic_slice_in_dim(latents, sec * SLICE, SLICE, axis=2)
-    gain = lax.dynamic_slice_in_dim(norm_gain[0], seq * part, part)[:, None]
-    scale = jnp.where(jnp.arange(3 * dim) < dim, HEAD_DIM ** (-0.5) * math.log2(math.e), 1.0).astype(F32)
-    folded = (qkv_weight[0].astype(F32) * gain * scale[None, :]).astype(BF16)
-    packed = jnp.concatenate([folded, proj_weight[0]], axis=1)
-    packed = packed.reshape(part, 4, ns, SLICE).transpose(2, 0, 1, 3).reshape(ns, part, 4 * SLICE)
-    merges = merge_weight[0].reshape(part, ns, SLICE).transpose(1, 0, 2)
     dma = pltpu.SemaphoreType.DMA
     vmem = pl.BlockSpec(memory_space=pltpu.VMEM)
     gather_sems = [dma((2,)), dma((2,))]
@@ -399,9 +441,17 @@
     return pl.pallas_call(
         functools.partial(kernel, ns, ny, nz, tok),
         out_shape=jax.ShapeDtypeStruct((nz, tok, SLICE), BF16),
-        in_specs=[vmem] * 4,
+        in_specs=[pl.BlockSpec(memory_space=pltpu.MemorySpace.HBM)] * 5,
         out_specs=vmem,
         scratch_shapes=[
+            pltpu.VMEM((nz, tok, SLICE), BF16),
+            pltpu.VMEM((1, dim), F32),
+            pltpu.VMEM((part, 3 * dim), BF16),
+            pltpu.VMEM((part, dim), BF16),
+            pltpu.VMEM((part, dim), BF16),
+            dma((5,)),
+            pltpu.VMEM((ns, part, 4 * SLICE), BF16),
+            pltpu.VMEM((ns, part, SLICE), BF16),
             pltpu.VMEM((2, ns, half, SLICE), BF16),
             pltpu.VMEM((2, ns, half, SLICE), BF16),
             pltpu.VMEM((2, 2, CORES, ny, half, 2 * SLICE), BF16),
@@ -414,6 +464,7 @@
             dma((ns - 1,)), dma((ns,)),
             dma((ns - 1,)), dma((ns,)),
             dma((ns - 1,)), dma((mid,)),
+            dma((nz,)),
             *w_sems,
             *w_sems,
             *gather_sems,
@@ -421,9 +472,9 @@
             dma((2,)), dma((2, 2, ny)), dma((2, 2)), dma((2,)),
             dma((nz - 1,)), dma((nz,)),
         ],
-        compiler_params=pltpu.CompilerParams(collective_id=0, has_side_effects=True, vmem_limit_bytes=48 * 1024 * 1024),
+        compiler_params=pltpu.CompilerParams(collective_id=0, has_side_effects=True, vmem_limit_bytes=63 * 1024 * 1024),
         name="blocks",
-    )(lat, packed, merges, proj_weight[0])
+    )(latents, norm_gain, qkv_weight[0], proj_weight[0], merge_weight[0])
 
 
 def solution(mesh):

time: 211 us -> 208 us (0.986)
  no operation moved by 1% of the time
where the time goes in v4:
time: 208 us; the launch traced here: 207 us
  Pallas kernels  205 us (99%)
    pallas_call x1, Pallas kernels, body(): pl.pallas_call(functools.partial(kernel, ns, ny, nz, tok), out_shape=jax....  205 us

profile of v4, /device:TPU:8, one launch (start us, length us, event | category | flops | bytes accessed | tf_op | source)
XLA Modules:
  0.0 207.0 jit_solution(6580199284336701159)
XLA Ops:
  0.0 205.5 %blocks.1 = bf16[4,64,128]{2,1,0:T(8,128)(2,1)} custom-call(bf16[4,64,1024]{2,1,0:T(8,128)(2,1)} %lat_hbm.1, f32[1,1024]{1,0:T(1,128)} %gain_hbm.1, bf16[32,3072]{1,0:T(8,128)(2,1)} %bitcast.3, bf16[32,1024]{1,0:T(8,128)(2,1)} %bitcast.4, bf16[32,1024]{1,0:T(8,128)(2,1)} %bitcast.5), custom_call_target="tpu_custom_call" | custom-call | tf_op jit(solution)/shard_map/blocks/pallas_call | solution.py:441
  205.5 1.5 copy.7

commit v5 on v4

--- a/solution.py
+++ b/solution.py
@@ -65,15 +65,18 @@
     farthest = [(dx, dz) for dx in range(nx) for dz in range(2) if (dx, dz) != (0, 0)]
     farthest.sort(key=lambda o: -(min(o[0], nx - o[0]) + o[1]))
 
+    sec_peers = [None] + [lax.rem(sec // nx + dz, 2) * nx + lax.rem(sec + dx, nx) for dx, dz in farthest]
+    z_peers = [lax.rem(z + d, nz) for d in range(nz)]
+    y_peers = [lax.rem(y + d, ny) for d in range(ny)]
+
     def sec_peer(d):
-        dx, dz = farthest[d - 1]
-        return lax.rem(sec // nx + dz, 2) * nx + lax.rem(sec + dx, nx)
+        return sec_peers[d]
 
     def z_peer(d):
-        return lax.rem(z + d, nz)
+        return z_peers[d]
 
     def y_peer(d):
-        return lax.rem(y + d, ny)
+        return y_peers[d]
 
     y_order = sorted(range(1, ny), key=lambda d: -min(d, ny - d))
     sibling = seq_of(y, z, 1 - c)
@@ -299,10 +302,6 @@
     def block(s, carry):
         par = lax.rem(s, 2)
         c_wait(W, w_sems, s)
-
-        @pl.when((s >= 1) & (s <= mid))
-        def _():
-            c_wait(MD, m_sems, s - 1)
 
         stacked = []
         for g in range(2):
@@ -326,6 +325,10 @@
 
         prefetch_z(s)
 
+        @pl.when((s >= 1) & (s <= mid))
+        def _():
+            c_wait(MD, m_sems, s - 1)
+
         @pl.when((s == 0) & composed)
         def _():
             start(proj_copies())
@@ -361,9 +364,9 @@
 
         tops, sums, mixes = [None, None], [None, None], [None, None]
 
-        def attend(gq, g, core):
-            keys = KV[par, g, core, :, :, 0:SLICE].reshape(ny * half, SLICE)
-            vals = KV[par, g, core, :, :, SLICE:2 * SLICE].reshape(ny * half, SLICE)
+        def attend(gq, g, cores):
+            keys = jnp.concatenate([KV[par, g, core, :, :, 0:SLICE].reshape(ny * half, SLICE) for core in cores], axis=0)
+            vals = jnp.concatenate([KV[par, g, core, :, :, SLICE:2 * SLICE].reshape(ny * half, SLICE) for core in cores], axis=0)
             scores = lax.dot_general(stacked[gq], keys, (((1,), (1,)), ((), ())), preferred_element_type=F32)
             top = jnp.max(scores, axis=-1, keepdims=True)
             if tops[gq] is not None:
@@ -380,15 +383,13 @@
         for g in range(2):
             for d in reversed(y_order):
                 kv_relay(par, g, d)
-            for gq in range(2):
-                attend(gq, g, c)
             if g == 1:
                 prefetch(stage_y, s)
                 for half_ in range(2):
                     gather_all(H, hs, hr, half_).wait_send()
             kv_other(par, g)
             for gq in range(2):
-                attend(gq, g, 1 - c)
+                attend(gq, g, [0, 1])
                 if g == 1:
                     mix = mixes[gq] / sums[gq]
                     A[gq, sec] = jnp.where(lane < HEAD_DIM, mix[:half], mix[half:]).astype(BF16)

time: 208 us -> 206 us (level)
  no operation moved by 1% of the time
where the time goes in v5:
time: 206 us
  Pallas kernels  205 us (100%)
    pallas_call x1, Pallas kernels, body(): pl.pallas_call(functools.partial(kernel, ns, ny, nz, tok), out_shape=jax....  205 us

profile of v5, /device:TPU:8, one launch (start us, length us, event | category | flops | bytes accessed | tf_op | source)
XLA Modules:
  0.0 206.1 jit_solution(2643155652799142422)
XLA Ops:
  0.0 204.6 %blocks.1 = bf16[4,64,128]{2,1,0:T(8,128)(2,1)} custom-call(bf16[4,64,1024]{2,1,0:T(8,128)(2,1)} %lat_hbm.1, f32[1,1024]{1,0:T(1,128)} %gain_hbm.1, bf16[32,3072]{1,0:T(8,128)(2,1)} %bitcast.3, bf16[32,1024]{1,0:T(8,128)(2,1)} %bitcast.4, bf16[32,1024]{1,0:T(8,128)(2,1)} %bitcast.5), custom_call_target="tpu_custom_call" | custom-call | tf_op jit(solution)/shard_map/blocks/pallas_call | solution.py:442
  204.6 1.5 copy.7

commit v6 on v5

--- a/solution.py
+++ b/solution.py
@@ -301,7 +301,6 @@
     lane = lax.broadcasted_iota(jnp.int32, (half, SLICE), 1)
     def block(s, carry):
         par = lax.rem(s, 2)
-        c_wait(W, w_sems, s)
 
         stacked = []
         for g in range(2):
@@ -317,6 +316,8 @@
             spread = jnp.sum(total, axis=-1, keepdims=True) * (1.0 / dim)
             inverse = lax.rsqrt(spread + EPSILON)
             normed = jnp.concatenate([((H[g, p].astype(F32) - mean) * inverse).astype(BF16) for p in range(ns)], axis=1)
+            if g == 0:
+                c_wait(W, w_sems, s)
             kv = jnp.dot(normed, weights(s, 128, 384), preferred_element_type=F32)
             KV[par, g, c, y] = kv.astype(BF16)
             kv_start(par, g)

time: 206 us -> 206 us (level)
  no operation moved by 1% of the time
where the time goes in v6:
time: 206 us; the launch traced here: 205 us
  Pallas kernels  204 us (99%)
    pallas_call x1, Pallas kernels, body(): pl.pallas_call(functools.partial(kernel, ns, ny, nz, tok), out_shape=jax....  204 us

profile of v6, /device:TPU:8, one launch (start us, length us, event | category | flops | bytes accessed | tf_op | source)
XLA Modules:
  0.0 205.1 jit_solution(12778650863955448729)
XLA Ops:
  0.0 203.6 %blocks.1 = bf16[4,64,128]{2,1,0:T(8,128)(2,1)} custom-call(bf16[4,64,1024]{2,1,0:T(8,128)(2,1)} %lat_hbm.1, f32[1,1024]{1,0:T(1,128)} %gain_hbm.1, bf16[32,3072]{1,0:T(8,128)(2,1)} %bitcast.3, bf16[32,1024]{1,0:T(8,128)(2,1)} %bitcast.4, bf16[32,1024]{1,0:T(8,128)(2,1)} %bitcast.5), custom_call_target="tpu_custom_call" | custom-call | tf_op jit(solution)/shard_map/blocks/pallas_call | solution.py:443
  203.6 1.5 copy.7
